TPU v7x, 512 devices: a whole 4x4x16 slice. The times are simulated.
512 devices in a mesh: gx: 8 (over y, core), gy: 16 (over z), grp: 4 (over x).
Axes of the slice: x: 4, y: 4, z: 16, core: 2. Of those that a mesh axis runs over, the one named last changes fastest.
Arguments:
- rhs: bfloat16 [4096, 64, 128], P(('gx', 'gy', 'grp')), may hold values from -6 to 6
- element_blocks: float32 [4096, 64, 448], P(('gx', 'gy', 'grp')), may hold values from -2 to 16
- element_table: int32 [4096, 6], P(('gx', 'gy', 'grp')), may hold values from -1 to 23, as said below
- element_block_inverses: float32 [4096, 64, 64], P(('gx', 'gy', 'grp')), may hold values from -1 to 2
- basis: float32 [4096, 64, 8], P(('gx', 'gy', 'grp')), may hold values from -0.75 to 0.75
- element_aggregate: int32 [4096], P(('gx', 'gy', 'grp')), may hold values from 0 to 1, as said below
- aggregate_blocks: float32 [1024, 8, 56], P(('gx', 'gy', 'grp')), may hold values from -2 to 16
- aggregate_table: int32 [1024, 6], P(('gx', 'gy', 'grp')), may hold values from -1 to 5, as said below
- aggregate_inverse: float32 [1024, 8, 8], P(('gx', 'gy', 'grp')), may hold values from -1 to 2
- coarse_map: int32 [1024], P(('gx', 'gy', 'grp')), may hold values from 0 to 7, as said below
- coarse_owner: int32 [128, 8], P(('gx', 'gy')), may hold values from 0 to 3, as said below
- coarse_inverse: float32 [128, 64, 64], P(('gx', 'gy')), may hold values from -1 to 2
Outputs:
- solution: float32 [4096, 64, 128], P(('gx', 'gy', 'grp'))
- new_residual: float32 [4096, 64, 128], P(('gx', 'gy', 'grp'))
Inputs may be any that keep to these rules, and one draw needn't show every extreme that they name: `element_table`: row e of a device lists its neighbours across the faces -x, +x, -y, +y, -z, +z. A value t below 8 names element t of the previous device along gx+gy+grp, one below 16 element t - 8 of the same device, one from 16 on element t - 16 of the next device, and -1 no neighbour. Only column 0 names the previous device and only column 1 the next; on every device that has a previous one, exactly 4 of its rows name it, all different elements, and likewise for the next one. Neighbourhood is mutual. `element_aggregate`: each aggregate of a device holds 4 of its elements. `aggregate_table`: as for element_table, with 2 in place of 8 and 2 rows naming each neighbouring device. `coarse_map`: each of the 8 coarsest aggregates of a group gathers exactly 1 aggregate. `coarse_owner`: in every group one device owns exactly 4 coarsest aggregates and none owns more.
All inputs are finite; a program needn't handle non-finite values.
Results may differ from a plain program's by a relative error of at most 0.0003.
Values sent between devices are 32-bit elements; how exact they have to be, the bound alone decides.
A program may use at most 64 MiB of HBM per device.

v0:
```python
import jax
import jax.numpy as jnp
from jax import lax
from jax.sharding import PartitionSpec as P

OMEGA = 0.7
LOW_BOUND = 0.25
UPPER_LIMIT = 1.9
TOP_PRECISION = lax.Precision.HIGHEST


def padded(block, sides, width):
    for axis, dim in sides:
        count = lax.axis_size(axis)
        forward = [(i, i + 1) for i in range(count - 1)]
        backward = [(target, source) for source, target in forward]
        low = lax.ppermute(
            lax.slice_in_dim(block, block.shape[dim] - width, None, axis=dim), axis, forward
        )
        high = lax.ppermute(lax.slice_in_dim(block, 0, width, axis=dim), axis, backward)
        block = jnp.concatenate([low, block, high], axis=dim)
    return block


def chebyshev(apply_matrix, apply_inverse, right, start):
    theta = (UPPER_LIMIT + LOW_BOUND) / 2.0
    delta = (UPPER_LIMIT - LOW_BOUND) / 2.0
    sigma = theta / delta
    rho = 1.0 / sigma
    if start is None:
        update = apply_inverse(right)
        answer = jnp.zeros_like(right)
    else:
        update = apply_inverse(right - apply_matrix(start))
        answer = start
    direction = update / theta
    answer = answer + direction
    for repeat_step in range(2):
        update = update - apply_inverse(apply_matrix(direction))
        rho_next = 1.0 / (2.0 * sigma - rho)
        direction = rho_next * rho * direction + 2.0 * rho_next / delta * update
        answer = answer + direction
        rho = rho_next
    return answer


def stacked_product(blocks, field, window, neighbours):
    gathered = window[neighbours]
    stacked = jnp.concatenate([field[:, None], gathered], axis=1)
    stacked = stacked.reshape(field.shape[0], 7 * field.shape[1], field.shape[2])
    return jnp.einsum("eij,ejr->eir", blocks, stacked, precision=TOP_PRECISION)


def inverse_product(inverses, vector):
    return jnp.einsum("eij,ejr->eir", inverses, vector, precision=TOP_PRECISION)


def on_device(
    rhs,
    element_blocks,
    element_table,
    element_block_inverses,
    basis,
    element_aggregate,
    aggregate_blocks,
    aggregate_table,
    aggregate_inverse,
    coarse_map,
    coarse_owner,
    coarse_inverse,
):
    elements = rhs.shape[0]
    aggregates = aggregate_table.shape[0]
    modes = basis.shape[2]
    columns = rhs.shape[2]
    fine_blank = jnp.zeros((1,) + rhs.shape[1:], jnp.float32)
    middle_blank = jnp.zeros((1, modes, columns), jnp.float32)
    fine_table = jnp.where(element_table < 0, 3 * elements, element_table)
    middle_table = jnp.where(aggregate_table < 0, 3 * aggregates, aggregate_table)

    def fine_matrix(vector):
        extended = padded(vector, ((("gx", "gy", "grp"), 0),), elements)
        window = jnp.concatenate([extended, fine_blank], axis=0)
        return stacked_product(element_blocks, vector, window, fine_table)

    def fine_inverse(vector):
        return inverse_product(element_block_inverses, vector)

    def middle_matrix(vector):
        extended = padded(vector, ((("gx", "gy", "grp"), 0),), aggregates)
        window = jnp.concatenate([extended, middle_blank], axis=0)
        return stacked_product(aggregate_blocks, vector, window, middle_table)

    def middle_inverse(vector):
        return inverse_product(aggregate_inverse, vector)

    residual = rhs.astype(jnp.float32)
    presmooth = chebyshev(fine_matrix, fine_inverse, residual, None)
    defect = residual - fine_matrix(presmooth)
    smoothed = defect - OMEGA * fine_matrix(fine_inverse(defect))
    projected = jnp.einsum("epk,epr->ekr", basis, smoothed, precision=TOP_PRECISION)
    member = (
        element_aggregate[None, :] == jnp.arange(aggregates, dtype=jnp.int32)[:, None]
    ).astype(jnp.float32)
    residual_one = jnp.einsum("ae,ekr->akr", member, projected, precision=TOP_PRECISION)
    pre_one = chebyshev(middle_matrix, middle_inverse, residual_one, None)
    defect_one = residual_one - middle_matrix(pre_one)
    coarse_count = coarse_owner.shape[1]
    belongs = (coarse_map[None, :] == jnp.arange(coarse_count, dtype=jnp.int32)[:, None]).astype(
        jnp.float32
    )
    partial_rhs = jnp.einsum("ca,akr->ckr", belongs, defect_one, precision=TOP_PRECISION)
    coarse_right_side = lax.psum(partial_rhs, "grp").reshape(coarse_count * modes, columns)
    owners = coarse_owner[0]
    inverse = coarse_inverse[0]
    owner_rows = jnp.repeat(owners, modes)
    myself = lax.axis_index("grp")
    owned_here = (owners == myself).astype(jnp.int32)
    picked = jnp.argsort(1 - owned_here, stable=True)[: lax.axis_size("grp")]
    valid_rows = owned_here[picked].astype(jnp.float32)
    rows_owned = inverse.reshape(coarse_count, modes, coarse_count * modes)[picked]
    rows_owned = jnp.where((owner_rows == myself)[None, None, :], rows_owned, 0.0)
    local_part = jnp.einsum("mkn,nr->mkr", rows_owned, coarse_right_side, precision=TOP_PRECISION)
    placing = (picked[:, None] == jnp.arange(coarse_count, dtype=jnp.int32)[None, :]).astype(
        jnp.float32
    )
    placing = placing * valid_rows[:, None]
    placed = jnp.einsum("mc,mkr->ckr", placing, local_part, precision=TOP_PRECISION)
    coarse_answer_vector = lax.psum(placed, "grp")
    lift_one = jnp.einsum("ca,ckr->akr", belongs, coarse_answer_vector, precision=TOP_PRECISION)
    post_one = chebyshev(middle_matrix, middle_inverse, residual_one, pre_one + lift_one)
    spread_values = jnp.einsum("ae,akr->ekr", member, post_one, precision=TOP_PRECISION)
    lifted = jnp.einsum("epk,ekr->epr", basis, spread_values, precision=TOP_PRECISION)
    correction = lifted - OMEGA * fine_inverse(fine_matrix(lifted))
    precond = chebyshev(fine_matrix, fine_inverse, residual, presmooth + correction)
    numerator = lax.psum(jnp.sum(residual * precond, axis=(0, 1)), ("gx", "gy", "grp"))
    applied = fine_matrix(precond)
    denominator = lax.psum(jnp.sum(precond * applied, axis=(0, 1)), ("gx", "gy", "grp"))
    step_size = numerator / denominator
    return (step_size * precond, residual - step_size * applied)


def solution(mesh):
    return jax.shard_map(
        on_device,
        mesh=mesh,
        in_specs=(
            P(("gx", "gy", "grp"), None, None),
            P(("gx", "gy", "grp"), None, None),
            P(("gx", "gy", "grp"), None),
            P(("gx", "gy", "grp"), None, None),
            P(("gx", "gy", "grp"), None, None),
            P(("gx", "gy", "grp")),
            P(("gx", "gy", "grp"), None, None),
            P(("gx", "gy", "grp"), None),
            P(("gx", "gy", "grp"), None, None),
            P(("gx", "gy", "grp")),
            P(("gx", "gy"), None),
            P(("gx", "gy"), None, None),
        ),
        out_specs=(P(("gx", "gy", "grp"), None, None), P(("gx", "gy", "grp"), None, None)),
        check_vma=False,
    )
```

profile of v0, /device:TPU:1, one launch (start us, length us, event | category | flops | bytes accessed | tf_op | source)
XLA Modules:
  0.0 421.2 jit_solution(16344840261081103723)
XLA Ops:
  3.4 14.7 %collective-permute-start.1 = (f32[8,64,128]{2,1,0:T(8,128)S(1)}, f32[8,64,128]{2,1,0:T(8,128)S(1)}, u32[]{:S(2)}, u32[]{:S(2)}) collective-permute-start(f32[8,64,128]{2,1,0:T(8,128)S(1)} %get-tuple-element.15), channel_id=1, source_target_pairs={{1,0},{2,1},{3,2},{4,3},{5,4},{6,5},{7,6},{8,7},{9,8},{10,9},{11,1... | collective-permute-start | bytes 786440 | tf_op jit(solution)/shard_map/ppermute | solution.py:20
  18.1 1.9 collective-permute-start
  21.4 10.5 %collective-permute-done = f32[8,64,128]{2,1,0:T(8,128)S(1)} collective-permute-done((f32[8,64,128]{2,1,0:T(8,128)S(1)}, f32[8,64,128]{2,1,0:T(8,128)S(1)}, u32[]{:S(2)}, u32[]{:S(2)}) %collective-permute-start) | collective-permute-done | bytes 262176 | tf_op jit(solution)/shard_map/ppermute | solution.py:17
  35.8 1.9 collective-permute-start.3
  37.7 3.4 collective-permute-start.2
  42.9 7.7 %collective-permute-done.2 = f32[8,64,128]{2,1,0:T(8,128)S(1)} collective-permute-done((f32[8,64,128]{2,1,0:T(8,128)S(1)}, f32[8,64,128]{2,1,0:T(8,128)S(1)}, u32[]{:S(2)}, u32[]{:S(2)}) %collective-permute-start.2) | collective-permute-done | bytes 262176 | tf_op jit(solution)/shard_map/ppermute | solution.py:17
  56.2 1.9 collective-permute-start.5
  58.2 3.4 collective-permute-start.4
  61.6 4.8 %collective-permute-done.5 = f32[8,64,128]{2,1,0:T(8,128)S(1)} collective-permute-done((f32[8,64,128]{2,1,0:T(8,128)S(1)}, f32[8,64,128]{2,1,0:T(8,128)S(1)}, u32[]{:S(2)}, u32[]{:S(2)}) %collective-permute-start.5) | collective-permute-done | bytes 262176 | tf_op jit(solution)/shard_map/ppermute | solution.py:20
  66.3 3.8 collective-permute-done.4
  70.2 1.8 gather_fusion.2
  75.6 1.9 collective-permute-start.7
  77.5 3.4 collective-permute-start.6
  82.8 5.8 %collective-permute-done.6 = f32[8,64,128]{2,1,0:T(8,128)} collective-permute-done((f32[8,64,128]{2,1,0:T(8,128)S(1)}, f32[8,64,128]{2,1,0:T(8,128)}, u32[]{:S(2)}, u32[]{:S(2)}) %collective-permute-start.6) | collective-permute-done | bytes 262176 | tf_op jit(solution)/shard_map/ppermute | solution.py:17
  89.7 1.8 gather_fusion.3
  95.4 1.9 collective-permute-start.9
  97.3 3.4 collective-permute-start.8
  101.7 3.9 collective-permute-done.8
  106.5 1.9 collective-permute-start.10
  108.5 7.0 %collective-permute-start.11 = (f32[2,8,128]{2,1,0:T(8,128)S(1)}, f32[2,8,128]{2,1,0:T(8,128)S(1)}, u32[]{:S(2)}, u32[]{:S(2)}) collective-permute-start(f32[2,8,128]{2,1,0:T(8,128)S(1)} %get-tuple-element.19), channel_id=1, source_target_pairs={{1,0},{2,1},{3,2},{4,3},{5,4},{6,5},{7,6},{8,7},{9,8},{10,9},{11,1... | collective-permute-start | bytes 24584 | tf_op jit(solution)/shard_map/ppermute | solution.py:20
  117.2 7.5 %collective-permute-start.13 = (f32[2,8,128]{2,1,0:T(8,128)S(1)}, f32[2,8,128]{2,1,0:T(8,128)S(1)}, u32[]{:S(2)}, u32[]{:S(2)}) collective-permute-start(f32[2,8,128]{2,1,0:T(8,128)S(1)} %fusion.23), channel_id=1, source_target_pairs={{1,0},{2,1},{3,2},{4,3},{5,4},{6,5},{7,6},{8,7},{9,8},{10,9},{11,1... | collective-permute-start | bytes 24584 | tf_op jit(solution)/shard_map/ppermute | solution.py:20
  124.7 1.9 collective-permute-start.12
  128.0 5.0 %collective-permute-done.12 = f32[2,8,128]{2,1,0:T(8,128)S(1)} collective-permute-done((f32[2,8,128]{2,1,0:T(8,128)S(1)}, f32[2,8,128]{2,1,0:T(8,128)S(1)}, u32[]{:S(2)}, u32[]{:S(2)}) %collective-permute-start.12) | collective-permute-done | bytes 8224 | tf_op jit(solution)/shard_map/ppermute | solution.py:17
  134.1 10.9 %psum.28 = f32[64,128]{1,0:T(8,128)S(1)} all-reduce(f32[64,128]{1,0:T(8,128)S(1)} %bitcast.305), channel_id=1, replica_groups=mesh['gx'=8,'gy'=16,'grp'=4] {'grp'}, use_global_device_ids=true, to_apply=%region_1.2 | all-reduce | flops 8192 | bytes 65536 | tf_op jit(solution)/shard_map/psum | solution.py:113
  145.5 12.3 %psum.29 = f32[8,8,128]{2,0,1:T(8,128)S(1)} all-reduce(f32[8,8,128]{2,0,1:T(8,128)S(1)} %fusion.52), channel_id=1, replica_groups=mesh['gx'=8,'gy'=16,'grp'=4] {'grp'}, use_global_device_ids=true, to_apply=%region_2.3 | all-reduce | flops 8192 | bytes 65536 | tf_op jit(solution)/shard_map/psum | solution.py:129
  158.0 9.4 %collective-permute-start.15 = (f32[2,8,128]{2,1,0:T(8,128)S(1)}, f32[2,8,128]{2,1,0:T(8,128)S(1)}, u32[]{:S(2)}, u32[]{:S(2)}) collective-permute-start(f32[2,8,128]{2,1,0:T(8,128)S(1)} %copy_add_fusion), channel_id=1, source_target_pairs={{1,0},{2,1},{3,2},{4,3},{5,4},{6,5},{7,6},{8,7},{9,8},{10,9},{11,1... | collective-permute-start | bytes 24584 | tf_op jit(solution)/shard_map/ppermute | solution.py:20
  167.4 1.9 collective-permute-start.14
  169.4 6.4 %collective-permute-done.14 = f32[2,8,128]{2,1,0:T(8,128)S(1)} collective-permute-done((f32[2,8,128]{2,1,0:T(8,128)S(1)}, f32[2,8,128]{2,1,0:T(8,128)S(1)}, u32[]{:S(2)}, u32[]{:S(2)}) %collective-permute-start.14) | collective-permute-done | bytes 8224 | tf_op jit(solution)/shard_map/ppermute | solution.py:17
  176.7 1.9 collective-permute-start.16
  178.6 7.0 %collective-permute-start.17 = (f32[2,8,128]{2,1,0:T(8,128)S(1)}, f32[2,8,128]{2,1,0:T(8,128)S(1)}, u32[]{:S(2)}, u32[]{:S(2)}) collective-permute-start(f32[2,8,128]{2,1,0:T(8,128)S(1)} %get-tuple-element.21), channel_id=1, source_target_pairs={{1,0},{2,1},{3,2},{4,3},{5,4},{6,5},{7,6},{8,7},{9,8},{10,9},{11,1... | collective-permute-start | bytes 24584 | tf_op jit(solution)/shard_map/ppermute | solution.py:20
  187.3 1.9 collective-permute-start.18
  189.2 7.5 %collective-permute-start.19 = (f32[2,8,128]{2,1,0:T(8,128)S(1)}, f32[2,8,128]{2,1,0:T(8,128)S(1)}, u32[]{:S(2)}, u32[]{:S(2)}) collective-permute-start(f32[2,8,128]{2,1,0:T(8,128)S(1)} %get-tuple-element.17), channel_id=1, source_target_pairs={{1,0},{2,1},{3,2},{4,3},{5,4},{6,5},{7,6},{8,7},{9,8},{10,9},{11,1... | collective-permute-start | bytes 24584 | tf_op jit(solution)/shard_map/ppermute | solution.py:20
  199.7 7.5 %collective-permute-start.21 = (f32[8,64,128]{2,1,0:T(8,128)S(1)}, f32[8,64,128]{2,1,0:T(8,128)S(1)}, u32[]{:S(2)}, u32[]{:S(2)}) collective-permute-start(f32[8,64,128]{2,1,0:T(8,128)S(1)} %bitcast.287), channel_id=1, source_target_pairs={{1,0},{2,1},{3,2},{4,3},{5,4},{6,5},{7,6},{8,7},{9,8},{10,9},{11,1... | collective-permute-start | bytes 786440 | tf_op jit(solution)/shard_map/ppermute | solution.py:20
  207.2 1.9 collective-permute-start.20
  210.5 7.7 %collective-permute-done.20 = f32[8,64,128]{2,1,0:T(8,128)S(1)} collective-permute-done((f32[8,64,128]{2,1,0:T(8,128)S(1)}, f32[8,64,128]{2,1,0:T(8,128)S(1)}, u32[]{:S(2)}, u32[]{:S(2)}) %collective-permute-start.20) | collective-permute-done | bytes 262176 | tf_op jit(solution)/shard_map/ppermute | solution.py:17
  223.8 1.9 collective-permute-start.23
  225.7 3.4 collective-permute-start.22
  230.9 5.8 %collective-permute-done.22 = f32[8,64,128]{2,1,0:T(8,128)S(1)} collective-permute-done((f32[8,64,128]{2,1,0:T(8,128)S(1)}, f32[8,64,128]{2,1,0:T(8,128)S(1)}, u32[]{:S(2)}, u32[]{:S(2)}) %collective-permute-start.22) | collective-permute-done | bytes 262176 | tf_op jit(solution)/shard_map/ppermute | solution.py:17
  242.2 1.9 collective-permute-start.24
  244.1 7.0 %collective-permute-start.25 = (f32[8,64,128]{2,1,0:T(8,128)S(1)}, f32[8,64,128]{2,1,0:T(8,128)S(1)}, u32[]{:S(2)}, u32[]{:S(2)}) collective-permute-start(f32[8,64,128]{2,1,0:T(8,128)S(1)} %get-tuple-element.13), channel_id=1, source_target_pairs={{1,0},{2,1},{3,2},{4,3},{5,4},{6,5},{7,6},{8,7},{9,8},{10,9},{11,1... | collective-permute-start | bytes 786440 | tf_op jit(solution)/shard_map/ppermute | solution.py:20
  251.1 2.1 collective-permute-done.24
  260.0 1.9 collective-permute-start.26
  261.9 7.7 %collective-permute-start.27 = (f32[8,64,128]{2,1,0:T(8,128)S(1)}, f32[8,64,128]{2,1,0:T(8,128)S(1)}, u32[]{:S(2)}, u32[]{:S(2)}) collective-permute-start(f32[8,64,128]{2,1,0:T(8,128)S(1)} %get-tuple-element.11), channel_id=1, source_target_pairs={{1,0},{2,1},{3,2},{4,3},{5,4},{6,5},{7,6},{8,7},{9,8},{10,9},{11,1... | collective-permute-start | bytes 786440 | tf_op jit(solution)/shard_map/ppermute | solution.py:20
  269.6 2.1 collective-permute-done.26
  278.5 7.7 %collective-permute-start.29 = (f32[8,64,128]{2,1,0:T(8,128)S(1)}, f32[8,64,128]{2,1,0:T(8,128)S(1)}, u32[]{:S(2)}, u32[]{:S(2)}) collective-permute-start(f32[8,64,128]{2,1,0:T(8,128)S(1)} %fusion.15), channel_id=1, source_target_pairs={{1,0},{2,1},{3,2},{4,3},{5,4},{6,5},{7,6},{8,7},{9,8},{10,9},{11,1... | collective-permute-start | bytes 786440 | tf_op jit(solution)/shard_map/ppermute | solution.py:20
  286.3 2.1 collective-permute-start.28
  289.6 7.7 %collective-permute-done.28 = f32[8,64,128]{2,1,0:T(8,128)S(1)} collective-permute-done((f32[8,64,128]{2,1,0:T(8,128)S(1)}, f32[8,64,128]{2,1,0:T(8,128)S(1)}, u32[]{:S(2)}, u32[]{:S(2)}) %collective-permute-start.28) | collective-permute-done | bytes 262176 | tf_op jit(solution)/shard_map/ppermute | solution.py:17
  302.3 118.1 %all-reduce = (f32[128]{0:T(128)S(1)}, f32[128]{0:T(128)S(1)}) all-reduce(f32[128]{0:T(128)S(1)} %get-tuple-element.5, f32[128]{0:T(128)S(1)} %get-tuple-element.4), channel_id=1, replica_groups=mesh['gx'=8,'gy'=16,'grp'=4] {'gx','gy','grp'}, use_global_device_ids=true, to_apply=%region_4.5 | all-reduce | flops 256 | bytes 2048 | tf_op jit(solution)/shard_map/psum | solution.py:136
  (148 shorter events, 72.7 us)
Async XLA Ops:
  0.6 33.2 %copy-start = (f32[8,64,448]{2,1,0:T(8,128)S(1)}, f32[8,64,448]{2,1,0:T(8,128)}, u32[]{:S(2)}) copy-start(f32[8,64,448]{2,1,0:T(8,128)} %param.13) | copy-start | bytes 2752516
  2.0 0.7 copy-start.2
  3.4 18.0 %collective-permute-start.1 = (f32[8,64,128]{2,1,0:T(8,128)S(1)}, f32[8,64,128]{2,1,0:T(8,128)S(1)}, u32[]{:S(2)}, u32[]{:S(2)}) collective-permute-start(f32[8,64,128]{2,1,0:T(8,128)S(1)} %get-tuple-element.15), channel_id=1, source_target_pairs={{1,0},{2,1},{3,2},{4,3},{5,4},{6,5},{7,6},{8,7},{9,8},{10,9},{11,1... | collective-permute-start | bytes 786440 | tf_op jit(solution)/shard_map/ppermute | solution.py:20
  18.1 13.8 %collective-permute-start = (f32[8,64,128]{2,1,0:T(8,128)S(1)}, f32[8,64,128]{2,1,0:T(8,128)S(1)}, u32[]{:S(2)}, u32[]{:S(2)}) collective-permute-start(f32[8,64,128]{2,1,0:T(8,128)S(1)} %get-tuple-element.15), channel_id=1, source_target_pairs={{0,1},{1,2},{2,3},{3,4},{4,5},{5,6},{6,7},{7,8},{8,9},{9,10},{10,1... | collective-permute-start | bytes 786440 | tf_op jit(solution)/shard_map/ppermute | solution.py:17
  33.8 1.6 copy-start.1
  33.8 1.6 copy-start.3
  35.8 7.1 %collective-permute-start.3 = (f32[8,64,128]{2,1,0:T(8,128)S(1)}, f32[8,64,128]{2,1,0:T(8,128)S(1)}, u32[]{:S(2)}, u32[]{:S(2)}) collective-permute-start(f32[8,64,128]{2,1,0:T(8,128)S(1)} %get-tuple-element.28), channel_id=1, source_target_pairs={{1,0},{2,1},{3,2},{4,3},{5,4},{6,5},{7,6},{8,7},{9,8},{10,9},{11,1... | collective-permute-start | bytes 786440 | tf_op jit(solution)/shard_map/ppermute | solution.py:20
  37.7 12.9 %collective-permute-start.2 = (f32[8,64,128]{2,1,0:T(8,128)S(1)}, f32[8,64,128]{2,1,0:T(8,128)S(1)}, u32[]{:S(2)}, u32[]{:S(2)}) collective-permute-start(f32[8,64,128]{2,1,0:T(8,128)S(1)} %get-tuple-element.28), channel_id=1, source_target_pairs={{0,1},{1,2},{2,3},{3,4},{4,5},{5,6},{6,7},{7,8},{8,9},{9,10},{10,1... | collective-permute-start | bytes 786440 | tf_op jit(solution)/shard_map/ppermute | solution.py:17
  54.2 7.3 %copy-start.10 = (s32[2,6]{1,0:T(2,128)S(1)}, s32[2,6]{1,0:T(2,128)}, u32[]{:S(2)}) copy-start(s32[2,6]{1,0:T(2,128)} %param.19) | copy-start | bytes 148
  56.2 10.1 %collective-permute-start.5 = (f32[8,64,128]{2,1,0:T(8,128)S(1)}, f32[8,64,128]{2,1,0:T(8,128)S(1)}, u32[]{:S(2)}, u32[]{:S(2)}) collective-permute-start(f32[8,64,128]{2,1,0:T(8,128)S(1)} %fusion.12), channel_id=1, source_target_pairs={{1,0},{2,1},{3,2},{4,3},{5,4},{6,5},{7,6},{8,7},{9,8},{10,9},{11,1... | collective-permute-start | bytes 786440 | tf_op jit(solution)/shard_map/ppermute | solution.py:20
  58.2 11.9 %collective-permute-start.4 = (f32[8,64,128]{2,1,0:T(8,128)S(1)}, f32[8,64,128]{2,1,0:T(8,128)S(1)}, u32[]{:S(2)}, u32[]{:S(2)}) collective-permute-start(f32[8,64,128]{2,1,0:T(8,128)S(1)} %fusion.12), channel_id=1, source_target_pairs={{0,1},{1,2},{2,3},{3,4},{4,5},{5,6},{6,7},{7,8},{8,9},{9,10},{10,1... | collective-permute-start | bytes 786440 | tf_op jit(solution)/shard_map/ppermute | solution.py:17
  72.0 1.6 copy-start.4
  73.6 7.3 %copy-start.11 = (s32[1,8]{1,0:T(1,128)S(1)}, s32[1,8]{1,0:T(1,128)}, u32[]{:S(2)}) copy-start(s32[1,8]{1,0:T(1,128)} %param.22) | copy-start | bytes 100
  75.6 7.2 %collective-permute-start.7 = (f32[8,64,128]{2,1,0:T(8,128)S(1)}, f32[8,64,128]{2,1,0:T(8,128)S(1)}, u32[]{:S(2)}, u32[]{:S(2)}) collective-permute-start(f32[8,64,128]{2,1,0:T(8,128)S(1)} %bitcast.294), channel_id=1, source_target_pairs={{1,0},{2,1},{3,2},{4,3},{5,4},{6,5},{7,6},{8,7},{9,8},{10,9},{11,1... | collective-permute-start | bytes 786440 | tf_op jit(solution)/shard_map/ppermute | solution.py:20
  77.5 11.1 %collective-permute-start.6 = (f32[8,64,128]{2,1,0:T(8,128)S(1)}, f32[8,64,128]{2,1,0:T(8,128)}, u32[]{:S(2)}, u32[]{:S(2)}) collective-permute-start(f32[8,64,128]{2,1,0:T(8,128)S(1)} %bitcast.295), channel_id=1, source_target_pairs={{0,1},{1,2},{2,3},{3,4},{4,5},{5,6},{6,7},{7,8},{8,9},{9,10},{10,1... | collective-permute-start | bytes 786440 | tf_op jit(solution)/shard_map/ppermute | solution.py:17
  93.1 1.6 copy-start.7
  93.1 2.0 copy-start.9
  93.1 2.1 copy-start.6
  93.1 13.1 %copy-start.5 = (f32[2,8,56]{2,1,0:T(8,128)S(1)}, f32[2,8,56]{2,1,0:T(8,128)}, u32[]{:S(2)}) copy-start(f32[2,8,56]{2,1,0:T(8,128)} %param.18) | copy-start | bytes 10756
  93.1 34.3 %copy-start.8 = (f32[1,64,64]{2,1,0:T(8,128)S(1)}, f32[1,64,64]{2,1,0:T(8,128)}, u32[]{:S(2)}) copy-start(f32[1,64,64]{2,1,0:T(8,128)} %param.23) | copy-start | bytes 49156
  93.1 40.6 %copy-start.12 = (s32[2]{0:T(128)S(1)}, s32[2]{0:T(128)}, u32[]{:S(2)}) copy-start(s32[2]{0:T(128)} %param.21) | copy-start | bytes 28
  95.4 6.4 %collective-permute-start.9 = (f32[2,8,128]{2,1,0:T(8,128)S(1)}, f32[2,8,128]{2,1,0:T(8,128)S(1)}, u32[]{:S(2)}, u32[]{:S(2)}) collective-permute-start(f32[2,8,128]{2,1,0:T(8,128)S(1)} %get-tuple-element.23), channel_id=1, source_target_pairs={{1,0},{2,1},{3,2},{4,3},{5,4},{6,5},{7,6},{8,7},{9,8},{10,9},{11,1... | collective-permute-start | bytes 24584 | tf_op jit(solution)/shard_map/ppermute | solution.py:20
  97.3 8.3 %collective-permute-start.8 = (f32[2,8,128]{2,1,0:T(8,128)S(1)}, f32[2,8,128]{2,1,0:T(8,128)S(1)}, u32[]{:S(2)}, u32[]{:S(2)}) collective-permute-start(f32[2,8,128]{2,1,0:T(8,128)S(1)} %get-tuple-element.23), channel_id=1, source_target_pairs={{0,1},{1,2},{2,3},{3,4},{4,5},{5,6},{6,7},{7,8},{8,9},{9,10},{10,1... | collective-permute-start | bytes 24584 | tf_op jit(solution)/shard_map/ppermute | solution.py:17
  106.5 8.9 %collective-permute-start.10 = (f32[2,8,128]{2,1,0:T(8,128)S(1)}, f32[2,8,128]{2,1,0:T(8,128)S(1)}, u32[]{:S(2)}, u32[]{:S(2)}) collective-permute-start(f32[2,8,128]{2,1,0:T(8,128)S(1)} %get-tuple-element.19), channel_id=1, source_target_pairs={{0,1},{1,2},{2,3},{3,4},{4,5},{5,6},{6,7},{7,8},{8,9},{9,10},{10,1... | collective-permute-start | bytes 24584 | tf_op jit(solution)/shard_map/ppermute | solution.py:17
  108.5 7.7 %collective-permute-start.11 = (f32[2,8,128]{2,1,0:T(8,128)S(1)}, f32[2,8,128]{2,1,0:T(8,128)S(1)}, u32[]{:S(2)}, u32[]{:S(2)}) collective-permute-start(f32[2,8,128]{2,1,0:T(8,128)S(1)} %get-tuple-element.19), channel_id=1, source_target_pairs={{1,0},{2,1},{3,2},{4,3},{5,4},{6,5},{7,6},{8,7},{9,8},{10,9},{11,1... | collective-permute-start | bytes 24584 | tf_op jit(solution)/shard_map/ppermute | solution.py:20
  117.2 10.8 %collective-permute-start.13 = (f32[2,8,128]{2,1,0:T(8,128)S(1)}, f32[2,8,128]{2,1,0:T(8,128)S(1)}, u32[]{:S(2)}, u32[]{:S(2)}) collective-permute-start(f32[2,8,128]{2,1,0:T(8,128)S(1)} %fusion.23), channel_id=1, source_target_pairs={{1,0},{2,1},{3,2},{4,3},{5,4},{6,5},{7,6},{8,7},{9,8},{10,9},{11,1... | collective-permute-start | bytes 24584 | tf_op jit(solution)/shard_map/ppermute | solution.py:20
  124.7 8.3 %collective-permute-start.12 = (f32[2,8,128]{2,1,0:T(8,128)S(1)}, f32[2,8,128]{2,1,0:T(8,128)S(1)}, u32[]{:S(2)}, u32[]{:S(2)}) collective-permute-start(f32[2,8,128]{2,1,0:T(8,128)S(1)} %fusion.23), channel_id=1, source_target_pairs={{0,1},{1,2},{2,3},{3,4},{4,5},{5,6},{6,7},{7,8},{8,9},{9,10},{10,1... | collective-permute-start | bytes 24584 | tf_op jit(solution)/shard_map/ppermute | solution.py:17
  158.0 11.4 %collective-permute-start.15 = (f32[2,8,128]{2,1,0:T(8,128)S(1)}, f32[2,8,128]{2,1,0:T(8,128)S(1)}, u32[]{:S(2)}, u32[]{:S(2)}) collective-permute-start(f32[2,8,128]{2,1,0:T(8,128)S(1)} %copy_add_fusion), channel_id=1, source_target_pairs={{1,0},{2,1},{3,2},{4,3},{5,4},{6,5},{7,6},{8,7},{9,8},{10,9},{11,1... | collective-permute-start | bytes 24584 | tf_op jit(solution)/shard_map/ppermute | solution.py:20
  167.4 8.3 %collective-permute-start.14 = (f32[2,8,128]{2,1,0:T(8,128)S(1)}, f32[2,8,128]{2,1,0:T(8,128)S(1)}, u32[]{:S(2)}, u32[]{:S(2)}) collective-permute-start(f32[2,8,128]{2,1,0:T(8,128)S(1)} %copy_add_fusion), channel_id=1, source_target_pairs={{0,1},{1,2},{2,3},{3,4},{4,5},{5,6},{6,7},{7,8},{8,9},{9,10},{10,1... | collective-permute-start | bytes 24584 | tf_op jit(solution)/shard_map/ppermute | solution.py:17
  176.7 8.9 %collective-permute-start.16 = (f32[2,8,128]{2,1,0:T(8,128)S(1)}, f32[2,8,128]{2,1,0:T(8,128)S(1)}, u32[]{:S(2)}, u32[]{:S(2)}) collective-permute-start(f32[2,8,128]{2,1,0:T(8,128)S(1)} %get-tuple-element.21), channel_id=1, source_target_pairs={{0,1},{1,2},{2,3},{3,4},{4,5},{5,6},{6,7},{7,8},{8,9},{9,10},{10,1... | collective-permute-start | bytes 24584 | tf_op jit(solution)/shard_map/ppermute | solution.py:17
  178.6 7.7 %collective-permute-start.17 = (f32[2,8,128]{2,1,0:T(8,128)S(1)}, f32[2,8,128]{2,1,0:T(8,128)S(1)}, u32[]{:S(2)}, u32[]{:S(2)}) collective-permute-start(f32[2,8,128]{2,1,0:T(8,128)S(1)} %get-tuple-element.21), channel_id=1, source_target_pairs={{1,0},{2,1},{3,2},{4,3},{5,4},{6,5},{7,6},{8,7},{9,8},{10,9},{11,1... | collective-permute-start | bytes 24584 | tf_op jit(solution)/shard_map/ppermute | solution.py:20
  187.3 9.4 %collective-permute-start.18 = (f32[2,8,128]{2,1,0:T(8,128)S(1)}, f32[2,8,128]{2,1,0:T(8,128)S(1)}, u32[]{:S(2)}, u32[]{:S(2)}) collective-permute-start(f32[2,8,128]{2,1,0:T(8,128)S(1)} %get-tuple-element.17), channel_id=1, source_target_pairs={{0,1},{1,2},{2,3},{3,4},{4,5},{5,6},{6,7},{7,8},{8,9},{9,10},{10,1... | collective-permute-start | bytes 24584 | tf_op jit(solution)/shard_map/ppermute | solution.py:17
  189.2 8.3 %collective-permute-start.19 = (f32[2,8,128]{2,1,0:T(8,128)S(1)}, f32[2,8,128]{2,1,0:T(8,128)S(1)}, u32[]{:S(2)}, u32[]{:S(2)}) collective-permute-start(f32[2,8,128]{2,1,0:T(8,128)S(1)} %get-tuple-element.17), channel_id=1, source_target_pairs={{1,0},{2,1},{3,2},{4,3},{5,4},{6,5},{7,6},{8,7},{9,8},{10,9},{11,1... | collective-permute-start | bytes 24584 | tf_op jit(solution)/shard_map/ppermute | solution.py:20
  199.7 10.8 %collective-permute-start.21 = (f32[8,64,128]{2,1,0:T(8,128)S(1)}, f32[8,64,128]{2,1,0:T(8,128)S(1)}, u32[]{:S(2)}, u32[]{:S(2)}) collective-permute-start(f32[8,64,128]{2,1,0:T(8,128)S(1)} %bitcast.287), channel_id=1, source_target_pairs={{1,0},{2,1},{3,2},{4,3},{5,4},{6,5},{7,6},{8,7},{9,8},{10,9},{11,1... | collective-permute-start | bytes 786440 | tf_op jit(solution)/shard_map/ppermute | solution.py:20
  207.2 11.0 %collective-permute-start.20 = (f32[8,64,128]{2,1,0:T(8,128)S(1)}, f32[8,64,128]{2,1,0:T(8,128)S(1)}, u32[]{:S(2)}, u32[]{:S(2)}) collective-permute-start(f32[8,64,128]{2,1,0:T(8,128)S(1)} %bitcast.288), channel_id=1, source_target_pairs={{0,1},{1,2},{2,3},{3,4},{4,5},{5,6},{6,7},{7,8},{8,9},{9,10},{10,1... | collective-permute-start | bytes 786440 | tf_op jit(solution)/shard_map/ppermute | solution.py:17
  223.8 7.1 %collective-permute-start.23 = (f32[8,64,128]{2,1,0:T(8,128)S(1)}, f32[8,64,128]{2,1,0:T(8,128)S(1)}, u32[]{:S(2)}, u32[]{:S(2)}) collective-permute-start(f32[8,64,128]{2,1,0:T(8,128)S(1)} %fusion.13), channel_id=1, source_target_pairs={{1,0},{2,1},{3,2},{4,3},{5,4},{6,5},{7,6},{8,7},{9,8},{10,9},{11,1... | collective-permute-start | bytes 786440 | tf_op jit(solution)/shard_map/ppermute | solution.py:20
  225.7 11.0 %collective-permute-start.22 = (f32[8,64,128]{2,1,0:T(8,128)S(1)}, f32[8,64,128]{2,1,0:T(8,128)S(1)}, u32[]{:S(2)}, u32[]{:S(2)}) collective-permute-start(f32[8,64,128]{2,1,0:T(8,128)S(1)} %fusion.13), channel_id=1, source_target_pairs={{0,1},{1,2},{2,3},{3,4},{4,5},{5,6},{6,7},{7,8},{8,9},{9,10},{10,1... | collective-permute-start | bytes 786440 | tf_op jit(solution)/shard_map/ppermute | solution.py:17
  242.2 11.0 %collective-permute-start.24 = (f32[8,64,128]{2,1,0:T(8,128)S(1)}, f32[8,64,128]{2,1,0:T(8,128)S(1)}, u32[]{:S(2)}, u32[]{:S(2)}) collective-permute-start(f32[8,64,128]{2,1,0:T(8,128)S(1)} %get-tuple-element.13), channel_id=1, source_target_pairs={{0,1},{1,2},{2,3},{3,4},{4,5},{5,6},{6,7},{7,8},{8,9},{9,10},{10,1... | collective-permute-start | bytes 786440 | tf_op jit(solution)/shard_map/ppermute | solution.py:17
  244.1 10.3 %collective-permute-start.25 = (f32[8,64,128]{2,1,0:T(8,128)S(1)}, f32[8,64,128]{2,1,0:T(8,128)S(1)}, u32[]{:S(2)}, u32[]{:S(2)}) collective-permute-start(f32[8,64,128]{2,1,0:T(8,128)S(1)} %get-tuple-element.13), channel_id=1, source_target_pairs={{1,0},{2,1},{3,2},{4,3},{5,4},{6,5},{7,6},{8,7},{9,8},{10,9},{11,1... | collective-permute-start | bytes 786440 | tf_op jit(solution)/shard_map/ppermute | solution.py:20
  260.0 11.8 %collective-permute-start.26 = (f32[8,64,128]{2,1,0:T(8,128)S(1)}, f32[8,64,128]{2,1,0:T(8,128)S(1)}, u32[]{:S(2)}, u32[]{:S(2)}) collective-permute-start(f32[8,64,128]{2,1,0:T(8,128)S(1)} %get-tuple-element.11), channel_id=1, source_target_pairs={{0,1},{1,2},{2,3},{3,4},{4,5},{5,6},{6,7},{7,8},{8,9},{9,10},{10,1... | collective-permute-start | bytes 786440 | tf_op jit(solution)/shard_map/ppermute | solution.py:17
  261.9 11.0 %collective-permute-start.27 = (f32[8,64,128]{2,1,0:T(8,128)S(1)}, f32[8,64,128]{2,1,0:T(8,128)S(1)}, u32[]{:S(2)}, u32[]{:S(2)}) collective-permute-start(f32[8,64,128]{2,1,0:T(8,128)S(1)} %get-tuple-element.11), channel_id=1, source_target_pairs={{1,0},{2,1},{3,2},{4,3},{5,4},{6,5},{7,6},{8,7},{9,8},{10,9},{11,1... | collective-permute-start | bytes 786440 | tf_op jit(solution)/shard_map/ppermute | solution.py:20
  278.5 11.0 %collective-permute-start.29 = (f32[8,64,128]{2,1,0:T(8,128)S(1)}, f32[8,64,128]{2,1,0:T(8,128)S(1)}, u32[]{:S(2)}, u32[]{:S(2)}) collective-permute-start(f32[8,64,128]{2,1,0:T(8,128)S(1)} %fusion.15), channel_id=1, source_target_pairs={{1,0},{2,1},{3,2},{4,3},{5,4},{6,5},{7,6},{8,7},{9,8},{10,9},{11,1... | collective-permute-start | bytes 786440 | tf_op jit(solution)/shard_map/ppermute | solution.py:20
  286.3 11.0 %collective-permute-start.28 = (f32[8,64,128]{2,1,0:T(8,128)S(1)}, f32[8,64,128]{2,1,0:T(8,128)S(1)}, u32[]{:S(2)}, u32[]{:S(2)}) collective-permute-start(f32[8,64,128]{2,1,0:T(8,128)S(1)} %fusion.15), channel_id=1, source_target_pairs={{0,1},{1,2},{2,3},{3,4},{4,5},{5,6},{6,7},{7,8},{8,9},{9,10},{10,1... | collective-permute-start | bytes 786440 | tf_op jit(solution)/shard_map/ppermute | solution.py:17
where the time goes:
time: 423 us; the launch traced here: 421 us
  blocking collectives  141 us (33%)
  starting transfers between devices  129 us (30%)
  waiting for transfers between devices  86.3 us (20%)
  matrix products  22.6 us (5%)
  local copies, waits for them, and re-layouts  21.1 us (5%)
  other arithmetic  19.6 us (5%)
    psum x1, blocking collectives, on_device(): lax.psum(jnp.sum(residual * precond, axis=(0, 1)), ('gx', 'gy', 'grp'))  118 us
    ppermute x15, starting transfers between devices, padded(): lax.ppermute(lax.slice_in_dim(block, 0, width, axis=dim), axis, backward)  92.6 us
    ppermute x15, waiting for transfers between devices, padded(): lax.ppermute(lax.slice_in_dim(block, block.shape[dim] - width, None, axis...  68.4 us
    ppermute x15, starting transfers between devices, padded(): lax.ppermute(lax.slice_in_dim(block, block.shape[dim] - width, None, axis...  36.2 us
    gather x15, local copies, waits for them, and re-layouts, stacked_product(): gathered = window[neighbours]  18.7 us
    ppermute x15, waiting for transfers between devices, padded(): lax.ppermute(lax.slice_in_dim(block, 0, width, axis=dim), axis, backward)  17.9 us
    dot_general x15, matrix products, stacked_product(): return jnp.einsum('eij,ejr->eir', blocks, stacked, precision=TOP_PRECISION)  15.3 us
    concatenate x9, other arithmetic, stacked_product(): stacked = jnp.concatenate([field[:, None], gathered], axis=1)  13.7 us
  transfers between devices with their start and end apart: 30, of which 24 were waited for; matrix products, arithmetic and copies ran while one was open for 1% of the time, Pallas kernels for 0%

commit v1 on v0

v1 whole, which is shorter than its diff:
```python
import functools

import jax
import jax.numpy as jnp
from jax import lax
from jax.experimental import pallas as pl
from jax.experimental.pallas import tpu as pltpu
from jax.sharding import PartitionSpec as P

OMEGA = 0.7
LOW_BOUND = 0.25
UPPER_LIMIT = 1.9
THETA = (UPPER_LIMIT + LOW_BOUND) / 2.0
DELTA = (UPPER_LIMIT - LOW_BOUND) / 2.0
SIGMA = THETA / DELTA
RHO = [1.0 / SIGMA]
for _ in range(2):
    RHO.append(1.0 / (2.0 * SIGMA - RHO[-1]))
KEEP = [0.0, RHO[1] * RHO[0], RHO[2] * RHO[1]]
TAKE = [1.0 / THETA, 2.0 * RHO[1] / DELTA, 2.0 * RHO[2] / DELTA]

ELEMS = 8
NODES = 64
MODES = 8
LOADS = 128
HALO = 4
REACH = 2
SPAN = 2 * REACH + 1
MESH = pl.DeviceIdType.MESH
HIGHEST = lax.Precision.HIGHEST
F32 = jnp.float32
BF16 = jnp.bfloat16


def dot(a, b):
    return jnp.dot(a, b, preferred_element_type=F32)


def exact(a, b):
    return jnp.dot(a, b, preferred_element_type=F32, precision=HIGHEST)


def three(v):
    high = v.astype(BF16)
    rest = v - high.astype(F32)
    middle = rest.astype(BF16)
    low = (rest - middle.astype(F32)).astype(BF16)
    return high, middle, low


def iota(shape, dim):
    return lax.broadcasted_iota(jnp.int32, shape, dim)


def kernel(
    sizes,
    table,
    member,
    coarse_table,
    coarse_map,
    owner,
    rhs,
    blocks,
    inverses,
    basis,
    coarse_blocks,
    coarse_inverses,
    group_inverse,
    x_out,
    applied_out,
    step_out,
    near,
    far,
    give,
    da,
    a,
    window,
    halo,
    update,
    direction,
    answer,
    acc,
    field,
    sent,
    landed,
    prolong,
    prolong_t,
    prolong_sent,
    prolong_landed,
    pack,
    packs,
    level,
    kmat,
    amat,
    cmat,
    dmat,
    strip,
    own_b,
    all_b,
    part,
    parts_near,
    total,
    parts_far,
    send_sem,
    recv_sem,
    pro_send,
    pro_recv,
    pack_send,
    pack_recv,
    b_send,
    b_recv,
    sum_send,
    sum_recv,
):
    ngx, ngy, ngrp = sizes
    groups = ngx * ngy
    devices = groups * ngrp
    wide = SPAN * ngrp * 16
    full = level.shape[0]
    gx, gy, grp = (lax.axis_index(name) for name in ("gx", "gy", "grp"))
    group = gx * ngy + gy
    me = group * ngrp + grp

    def place(index):
        return (index // (ngy * ngrp), (index // ngrp) % ngy, index % ngrp)

    before = place((me + devices - 1) % devices)
    after = place((me + 1) % devices)

    def gather_partner(i):
        offset = i // ngrp
        offset = jnp.where(offset > REACH, offset - SPAN, offset)
        to_group = (group + offset + groups) % groups
        to_grp = (grp + i) % ngrp
        slot = (REACH - offset) * ngrp + grp
        return (to_group // ngy, to_group % ngy, to_grp), slot

    near_count = ngx * ngrp
    near_rank = gx * ngrp + grp

    def near_partner(i):
        rank = (near_rank + i) % near_count
        return (rank // ngrp, gy, rank % ngrp)

    def far_partner(i):
        return (gx, (gy + i) % ngy, grp)

    barrier = pltpu.get_barrier_semaphore()

    def greet(partner, count):
        def body(i, carry):
            pl.semaphore_signal(barrier, inc=1, device_id=partner(i), device_id_type=MESH)
            return carry

        lax.fori_loop(1, count, body, 0)

    greet(lambda i: gather_partner(i)[0], SPAN * ngrp)
    greet(near_partner, near_count)
    greet(far_partner, ngy)
    greetings = (SPAN * ngrp - 1) + (near_count - 1) + (ngy - 1)

    for e in range(ELEMS):
        for k in range(6):
            t = table[e, k]
            here = (t >= ELEMS) & (t < 2 * ELEMS)
            near[e, k] = jnp.where(here, t - ELEMS, ELEMS)
        low, high = table[e, 0], table[e, 1]
        low_rank = jnp.int32(0)
        high_rank = jnp.int32(0)
        for other in range(ELEMS):
            t = table[other, 0]
            low_rank += ((t >= 0) & (t < low)).astype(jnp.int32)
            t = table[other, 1]
            high_rank += ((t >= 2 * ELEMS) & (t < high)).astype(jnp.int32)
        named = (low >= 0) & (low < ELEMS)
        far[e, 0] = jnp.where(named, jnp.minimum(low_rank, HALO - 1), 2 * HALO)
        far[e, 1] = jnp.where(high >= 2 * ELEMS, HALO + jnp.minimum(high_rank, HALO - 1), 2 * HALO)
    for side in range(2):
        chosen = [jnp.int32(0) for _ in range(HALO)]
        count = jnp.int32(0)
        for e in range(ELEMS):
            t = table[e, side]
            flag = (t >= 0) & (t < ELEMS) if side == 0 else t >= 2 * ELEMS
            chosen = [jnp.where(flag & (count == j), e, chosen[j]) for j in range(HALO)]
            count += flag.astype(jnp.int32)
        for j in range(HALO):
            give[side, j] = chosen[j]

    window[ELEMS] = jnp.zeros((NODES, 3 * LOADS), BF16)
    halo[2 * HALO] = jnp.zeros((NODES, 3 * LOADS), BF16)

    for e in range(ELEMS):
        spot = iota((MODES, LOADS), 1) == iota((MODES, LOADS), 0) + MODES * member[e]
        prolong[e] = exact(basis[e], spot.astype(F32))
    for side in range(2):
        prolong_sent[side] = sum(
            pltpu.roll(prolong[give[side, j]], 16 * j, 1) if j else prolong[give[side, j]]
            for j in range(HALO)
        )

    lanes = iota((8, 128), 1)
    for agg in range(2):
        row = iota((56, 128), 0)
        want = jnp.full((56, 128), 2 + agg, jnp.int32)
        for k in range(6):
            want = jnp.where(row // 8 == k + 1, coarse_table[agg, k], want)
        spot = iota((56, 128), 1) == want * 8 + row % 8
        t_rows = exact(coarse_blocks[agg], spot.astype(F32))
        small = iota((8, 128), 1) == iota((8, 128), 0) + 48 + 8 * agg
        d_rows = exact(coarse_inverses[agg], small.astype(F32))
        whole = coarse_map[agg]
        coarse_rows = group_inverse[whole]
        mine = owner[0, whole]
        kept = jnp.zeros((8, 64), F32)
        for c in range(8):
            same = (owner[0, c] == mine).astype(F32)
            kept = jnp.where(iota((8, 64), 1) // 8 == c, same, kept)
        shift = iota((64, 128), 1) == iota((64, 128), 0) + 64
        m_rows = exact(jnp.where(kept > 0.5, coarse_rows, 0.0), shift.astype(F32))
        s_rows = (lanes == iota((8, 128), 0) + 8 * whole).astype(F32)
        dt_rows = pltpu.roll(exact(coarse_inverses[agg], t_rows), 64, 1)
        first = jnp.where(lanes < 48, t_rows, jnp.where(lanes < 64, d_rows, m_rows))
        pack[8 * agg : 8 * agg + 8, 0:128] = first
        pack[8 * agg : 8 * agg + 8, 128:256] = jnp.where(lanes < 64, s_rows, dt_rows)

    for e in range(ELEMS):
        pieces = jnp.concatenate(three(inverses[e]), axis=0)
        o = dot(pieces, rhs[e])
        q = o[0:64] + (o[64:128] + o[128:192])
        update[e] = q
        d = q * TAKE[0]
        direction[e] = d
        answer[e] = d

    pl.semaphore_wait(barrier, greetings)

    def ring(source, target, send, recv, side):
        return pltpu.make_async_remote_copy(
            src_ref=source,
            dst_ref=target,
            send_sem=send,
            recv_sem=recv,
            device_id=before if side == 0 else after,
            device_id_type=MESH,
        )

    pending = []

    def exchange(k, source):
        copies = []
        for side in range(2):
            for j in range(HALO):
                sent[k, side, j] = source[give[side, j]]
            copy = ring(
                sent.at[k, side], landed.at[k, 1 - side], send_sem.at[k, side], recv_sem.at[k, side], side
            )
            copy.start()
            copies.append(copy)
            pending.append(copy)
        return copies

    def cut(source):
        for e in range(ELEMS):
            high, middle, low = three(source[e])
            window[e, :, 0:128] = high
            window[e, :, 128:256] = middle
            window[e, :, 256:384] = low

    def cut_halo(source, slot):
        high, middle, low = three(source)
        halo[slot, :, 0:128] = high
        halo[slot, :, 128:256] = middle
        halo[slot, :, 256:384] = low

    def products(matrix, stack):
        o = dot(matrix, stack[:, 0:256])
        p = dot(matrix[0:64], stack[:, 256:384])
        small = o[64:128, 128:256] + o[128:192, 0:128] + p
        return o[0:64, 0:128] + ((o[0:64, 128:256] + o[64:128, 0:128]) + small)

    def local_part(matrix, e):
        stack = jnp.concatenate([window[e]] + [window[near[e, k]] for k in range(6)], axis=0)
        return products(matrix[e], stack)

    def halo_part(matrix, e):
        stack = jnp.concatenate([halo[far[e, 0]], halo[far[e, 1]]], axis=0)
        return products(matrix[e, :, 64:192], stack)

    def apply(k, matrix, source, finish, between=None):
        copies = exchange(k, source)
        cut(source)
        for e in range(ELEMS):
            acc[e] = local_part(matrix, e)
        if between is not None:
            between()
        for copy in copies:
            copy.wait_recv()
        for side in range(2):
            for j in range(HALO):
                cut_halo(landed[k, side, j], side * HALO + j)
        for e in range(ELEMS):
            finish(e, acc[e] + halo_part(matrix, e))

    def prepare():
        for e in range(ELEMS):
            high, middle, low = three(blocks[e])
            a[e, 0:64] = high
            a[e, 64:128] = middle
            a[e, 128:192] = low
            high, middle, low = three(exact(inverses[e], blocks[e]))
            da[e, 0:64] = high
            da[e, 64:128] = middle
            da[e, 128:192] = low

    for side in range(2):
        copy = ring(
            prolong_sent.at[side], prolong_landed.at[1 - side], pro_send.at[side], pro_recv.at[side], side
        )
        copy.start()
        pending.append(copy)

    def gather(source, target, send, recv):
        own_slot = REACH * ngrp + grp

        def body(i, carry):
            device, slot = gather_partner(i)
            pltpu.make_async_remote_copy(
                src_ref=source,
                dst_ref=target.at[slot],
                send_sem=send,
                recv_sem=recv,
                device_id=device,
                device_id_type=MESH,
            ).start()
            return carry

        lax.fori_loop(1, SPAN * ngrp, body, 0)
        target[own_slot] = source[...]

    def wait_bytes(target, count, sem):
        pltpu.make_async_copy(target.at[pl.ds(0, count)], target.at[pl.ds(0, count)], sem).wait()

    gathered = SPAN * ngrp - 1

    def level_matrices():
        wait_bytes(packs, gathered, pack_recv)
        wait_bytes(packs, gathered, pack_send)
        rows_of = SPAN * ngrp
        for ref in (kmat, amat, cmat, dmat):
            ref[...] = jnp.zeros((full, full), F32)
        blank = jnp.zeros((16, full - 128), F32)

        def spread(rows, first, count, move):
            keep = (iota((16, 128), 1) >= first) & (iota((16, 128), 1) < first + count)
            rows = jnp.concatenate([jnp.where(keep, rows, 0.0), blank], axis=1)
            return pltpu.roll(rows, (move - first) % full, 1)

        for w in range(rows_of):
            one = packs[w, :, 0:128]
            two = packs[w, :, 128:256]
            here = slice(16 * w, 16 * w + 16)
            amat[here, :] = spread(one, 0, 48, 16 * (w - 1))
            dmat[here, :] = spread(one, 48, 16, 16 * w)
            kmat[here, :] = spread(two, 64, 48, 16 * (w - 1))
        for s in range(SPAN):
            parts = [packs[s * ngrp + j] for j in range(ngrp)]
            stacked = jnp.concatenate(parts, axis=0)
            coarse = stacked[:, 64:128]
            places = stacked[:, 128:192]
            block = lax.dot_general(
                coarse, places, (((1,), (1,)), ((), ())), preferred_element_type=F32, precision=HIGHEST
            )
            size = 16 * ngrp
            row = jnp.concatenate([block, jnp.zeros((size, full - size), F32)], axis=1)
            cmat[size * s : size * s + size, :] = pltpu.roll(row, size * s, 1) if s else row

    def smooth(rows):
        q = rows
        d = rows * TAKE[0]
        y = d
        for i in (1, 2):
            q = q - exact(d, kmat[...])
            d = KEEP[i] * d + TAKE[i] * q
            y = y + d
        return y

    def level_strip():
        first = (REACH * ngrp + grp - 1) * 16
        unit = (iota((48, full), 1) == iota((48, full), 0) + first).astype(F32)
        u = smooth(unit)
        v = exact(u, kmat[...])
        m = exact(unit - v, cmat[...])
        y = smooth(v + exact(m, amat[...]))
        strip[...] = m + exact(2.0 * u - y, dmat[...])

    def pre_finish(i):
        def finish(e, value):
            q = update[e] - value
            update[e] = q
            if i < 3:
                d = KEEP[i] * direction[e] + TAKE[i] * q
                direction[e] = d
                answer[e] = answer[e] + d
            else:
                field[e] = answer[e] + OMEGA * q

        return finish

    def first_between():
        gather(pack, packs, pack_send, pack_recv)

    copies = exchange(0, direction)
    gather(pack, packs, pack_send, pack_recv)
    prepare()
    cut(direction)
    for e in range(ELEMS):
        acc[e] = local_part(da, e)
    for copy in copies:
        copy.wait_recv()
    for side in range(2):
        for j in range(HALO):
            cut_halo(landed[0, side, j], side * HALO + j)
    for e in range(ELEMS):
        pre_finish(1)(e, acc[e] + halo_part(da, e))
    apply(1, da, direction, pre_finish(2), level_matrices)
    apply(2, da, direction, pre_finish(3), level_strip)

    big = jnp.concatenate([prolong[e] for e in range(ELEMS)], axis=0)
    prolong_t[...] = big.T[0:16]

    def restrict(e, value):
        acc[e] = rhs[e].astype(F32) - value

    apply(3, a, field, restrict)
    own_b[...] = exact(prolong_t[...], acc[...].reshape(ELEMS * NODES, LOADS))

    gather(own_b, all_b, b_send, b_recv)
    wait_bytes(all_b, gathered, b_recv)
    wait_bytes(all_b, gathered, b_send)
    values = all_b[...].reshape(wide, LOADS)
    padded = jnp.concatenate([values, jnp.zeros((full - wide, LOADS), F32)], axis=0)
    c = exact(strip[...], padded)

    blank = jnp.zeros((128 - 16, LOADS), F32)
    own_c = jnp.concatenate([c[16:32], blank], axis=0)
    for e in range(ELEMS):
        field[e] = exact(prolong[e], own_c)
    cut(field)
    pro = pending[2:4]
    for copy in (pro if False else []):
        copy.wait_recv()
    for side in range(2):
        ring(
            prolong_sent.at[side], prolong_landed.at[1 - side], pro_send.at[side], pro_recv.at[side], side
        ).wait_recv()
    for side in range(2):
        rows = c[0:16] if side == 0 else c[32:48]
        for j in range(HALO):
            above = [jnp.zeros((16 * j, LOADS), F32)] if j else []
            spot = jnp.concatenate(above + [rows, jnp.zeros((112 - 16 * j, LOADS), F32)], axis=0)
            cut_halo(exact(prolong_landed[side], spot), side * HALO + j)
    for e in range(ELEMS):
        w = local_part(da, e) + halo_part(da, e)
        direction[e] = w
        update[e] = update[e] - w
        answer[e] = answer[e] + field[e] - OMEGA * w

    def post_finish(i):
        def finish(e, value):
            if i == 0:
                q = update[e] + OMEGA * value
                d = TAKE[0] * q
            else:
                q = update[e] - value
                d = KEEP[i] * direction[e] + TAKE[i] * q
            update[e] = q
            direction[e] = d
            answer[e] = answer[e] + d

        return finish

    apply(4, da, direction, post_finish(0))
    apply(5, da, direction, post_finish(1))
    apply(6, da, direction, post_finish(2))

    sums = [jnp.zeros((8, LOADS), F32), jnp.zeros((8, LOADS), F32)]

    def last(e, value):
        x = answer[e]
        applied_out[e] = value
        x_out[e] = x
        r = rhs[e].astype(F32)
        sums[0] = sums[0] + jnp.sum((r * x).reshape(8, 8, LOADS), axis=0)
        sums[1] = sums[1] + jnp.sum((x * value).reshape(8, 8, LOADS), axis=0)

    apply(7, a, answer, last)
    row = iota((8, LOADS), 0)
    numerator = jnp.sum(sums[0], axis=0, keepdims=True)
    denominator = jnp.sum(sums[1], axis=0, keepdims=True)
    part[...] = jnp.where(row == 0, numerator, jnp.where(row == 1, denominator, 0.0))

    def combine(source, target, partner, rank, count, which):
        def body(i, carry):
            pltpu.make_async_remote_copy(
                src_ref=source,
                dst_ref=target.at[rank],
                send_sem=sum_send.at[which],
                recv_sem=sum_recv.at[which],
                device_id=partner(i),
                device_id_type=MESH,
            ).start()
            return carry

        lax.fori_loop(1, count, body, 0)
        target[rank] = source[...]
        wait_bytes(target, count - 1, sum_recv.at[which])
        wait_bytes(target, count - 1, sum_send.at[which])
        return jnp.sum(target[...], axis=0)

    total[...] = combine(part, parts_near, near_partner, near_rank, near_count, 0)
    whole = combine(total, parts_far, far_partner, gy, ngy, 1)
    step_out[...] = jnp.broadcast_to(whole[0:1] / whole[1:2], (8, LOADS))
    for copy in pending:
        copy.wait_send()


def on_device(
    sizes,
    rhs,
    element_blocks,
    element_table,
    element_block_inverses,
    basis,
    element_aggregate,
    aggregate_blocks,
    aggregate_table,
    aggregate_inverse,
    coarse_map,
    coarse_owner,
    coarse_inverse,
):
    ngx, ngy, ngrp = sizes
    held = SPAN * ngrp
    full = -(-held * 16 // 128) * 128
    smem = pl.BlockSpec(memory_space=pltpu.SMEM)
    vmem = pl.BlockSpec(memory_space=pltpu.VMEM)
    shape = (ELEMS, NODES, LOADS)
    exchanges = 8
    scratch = [
        pltpu.SMEM((ELEMS, 6), jnp.int32),
        pltpu.SMEM((ELEMS, 2), jnp.int32),
        pltpu.SMEM((2, HALO), jnp.int32),
        pltpu.VMEM((ELEMS, 192, 448), BF16),
        pltpu.VMEM((ELEMS, 192, 448), BF16),
        pltpu.VMEM((ELEMS + 1, NODES, 3 * LOADS), BF16),
        pltpu.VMEM((2 * HALO + 1, NODES, 3 * LOADS), BF16),
        pltpu.VMEM(shape, F32),
        pltpu.VMEM(shape, F32),
        pltpu.VMEM(shape, F32),
        pltpu.VMEM(shape, F32),
        pltpu.VMEM(shape, F32),
        pltpu.VMEM((exchanges, 2, HALO, NODES, LOADS), F32),
        pltpu.VMEM((exchanges, 2, HALO, NODES, LOADS), F32),
        pltpu.VMEM(shape, F32),
        pltpu.VMEM((16, ELEMS * NODES), F32),
        pltpu.VMEM((2, NODES, LOADS), F32),
        pltpu.VMEM((2, NODES, LOADS), F32),
        pltpu.VMEM((16, 256), F32),
        pltpu.VMEM((held, 16, 256), F32),
        pltpu.VMEM((full, full), F32),
        pltpu.VMEM((full, full), F32),
        pltpu.VMEM((full, full), F32),
        pltpu.VMEM((full, full), F32),
        pltpu.VMEM((full, full), F32),
        pltpu.VMEM((48, full), F32),
        pltpu.VMEM((16, LOADS), F32),
        pltpu.VMEM((held, 16, LOADS), F32),
        pltpu.VMEM((8, LOADS), F32),
        pltpu.VMEM((ngx * ngrp, 8, LOADS), F32),
        pltpu.VMEM((8, LOADS), F32),
        pltpu.VMEM((ngy, 8, LOADS), F32),
        pltpu.SemaphoreType.DMA((exchanges, 2)),
        pltpu.SemaphoreType.DMA((exchanges, 2)),
        pltpu.SemaphoreType.DMA((2,)),
        pltpu.SemaphoreType.DMA((2,)),
        pltpu.SemaphoreType.DMA,
        pltpu.SemaphoreType.DMA,
        pltpu.SemaphoreType.DMA,
        pltpu.SemaphoreType.DMA,
        pltpu.SemaphoreType.DMA((2,)),
        pltpu.SemaphoreType.DMA((2,)),
    ]
    x, applied, step = pl.pallas_call(
        functools.partial(kernel, sizes),
        out_shape=(
            jax.ShapeDtypeStruct(shape, F32),
            jax.ShapeDtypeStruct(shape, F32),
            jax.ShapeDtypeStruct((8, LOADS), F32),
        ),
        in_specs=[smem] * 5 + [vmem] * 7,
        out_specs=(vmem, vmem, vmem),
        scratch_shapes=scratch,
        compiler_params=pltpu.CompilerParams(
            collective_id=0, has_side_effects=True, vmem_limit_bytes=48 * 1024 * 1024
        ),
    )(
        element_table,
        element_aggregate,
        aggregate_table,
        coarse_map,
        coarse_owner,
        rhs,
        element_blocks,
        element_block_inverses,
        basis,
        aggregate_blocks,
        aggregate_inverse,
        coarse_inverse.reshape(8, 8, 64),
    )
    step = step[0:1][None]
    return step * x, rhs.astype(F32) - step * applied


def solution(mesh):
    sizes = tuple(mesh.shape[name] for name in ("gx", "gy", "grp"))
    slabs = P(("gx", "gy", "grp"), None, None)
    pairs = P(("gx", "gy", "grp"), None)
    ids = P(("gx", "gy", "grp"))
    return jax.shard_map(
        functools.partial(on_device, sizes),
        mesh=mesh,
        in_specs=(
            slabs,
            slabs,
            pairs,
            slabs,
            slabs,
            ids,
            slabs,
            pairs,
            slabs,
            ids,
            P(("gx", "gy"), None),
            P(("gx", "gy"), None, None),
        ),
        out_specs=(slabs, slabs),
        check_vma=False,
    )
```

time: 423 us -> 99.7 us (0.24)
  blocking collectives: 141 us -> 0 us
  starting transfers between devices: 129 us -> 0 us
  Pallas kernels: 0 us -> 94.6 us
  waiting for transfers between devices: 86.3 us -> 0 us
  matrix products: 22.6 us -> 0 us
  other arithmetic: 19.6 us -> 0.85 us
  local copies, waits for them, and re-layouts: 21.1 us -> 3.19 us
    psum x3 -> x0, blocking collectives: 141 us -> none  [the longest x1 118 us: on_device(): lax.psum(jnp.sum(residual * precond, axis=(0, 1)), ('gx', 'gy', 'grp'))]
    ppermute x30 -> x0, starting transfers between devices: 129 us -> none  [the longest x15 92.6 us: padded(): lax.ppermute(lax.slice_in_dim(block, 0, width, axis=dim), axis, backward)]
    pallas_call x0 -> x1, Pallas kernels: none -> 94.6 us  [on_device(): pl.pallas_call(functools.partial(kernel, sizes), out_shape=(jax.ShapeDtyp...]
    ppermute x30 -> x0, waiting for transfers between devices: 86.3 us -> none  [the longest x15 68.4 us: padded(): lax.ppermute(lax.slice_in_dim(block, block.shape[dim] - width, None, axis...]
    dot_general x37 -> x0, matrix products: 22.6 us -> none  [the longest x15 15.3 us: stacked_product(): return jnp.einsum('eij,ejr->eir', blocks, stacked, precision=TOP_PRECISION)]
    gather x17 -> x0, local copies, waits for them, and re-layouts: 19.9 us -> none  [the longest x15 18.7 us: stacked_product(): gathered = window[neighbours]]
    concatenate x24 -> x0, other arithmetic: 16.1 us -> none  [the longest x9 13.7 us: stacked_product(): stacked = jnp.concatenate([field[:, None], gathered], axis=1)]
  transfers between devices with their start and end apart: 30 -> 0, of which waited for: 24 -> 0; matrix products, arithmetic and copies ran while one was open for 1% -> 0% of each run, Pallas kernels for 0% -> 0%
where the time goes in v1:
time: 99.7 us; the launch traced here: 99.4 us
  Pallas kernels  94.6 us (95%)
  local copies, waits for them, and re-layouts  3.19 us (3%)
    pallas_call x1, Pallas kernels, on_device(): pl.pallas_call(functools.partial(kernel, sizes), out_shape=(jax.ShapeDtyp...  94.6 us
    unnamed x23, local copies, waits for them, and re-layouts  3.19 us

profile of v1, /device:TPU:1, one launch (start us, length us, event | category | flops | bytes accessed | tf_op | source)
XLA Modules:
  0.0 99.4 jit_solution(5507942351824389084)
XLA Ops:
  0.6 0.0 copy-start.1
  0.6 0.0 copy-start.3
  0.7 0.0 copy-start.4
  0.7 0.0 copy-start.5
  0.7 0.0 copy-start.6
  0.7 0.0 copy-start.7
  0.7 0.0 copy-start.8
  0.7 0.0 copy-start.9
  0.7 0.0 copy-start.10
  0.7 1.0 copy.14.basis
  1.7 0.0 copy-done.1
  1.7 0.0 copy-done.3
  1.7 0.0 copy-done.4
  1.7 0.0 copy-done.5
  1.7 0.0 copy-done.6
  1.8 0.0 copy-done.7
  1.8 0.0 copy-done.8
  1.8 0.0 copy-done.9
  1.8 0.0 copy-done.10
  1.8 0.0 copy-start
  1.8 1.2 %copy-done = f32[8,64,448]{2,1,0:T(8,128)S(1)} copy-done((f32[8,64,448]{2,1,0:T(8,128)S(1)}, f32[8,64,448]{2,1,0:T(8,128)}, u32[]{:S(2)}) %copy-start) | copy-done | bytes 917528
  3.0 0.0 copy-start.2
  3.0 0.9 copy-done.2
  4.0 94.6 %shard_map.131 = (f32[8,64,128]{2,1,0:T(8,128)S(1)}, f32[8,64,128]{2,1,0:T(8,128)S(1)}, f32[8,128]{1,0:T(8,128)S(1)}) custom-call(s32[8,6]{1,0:T(8,128)S(1)} %copy-done.6, s32[8]{0:T(128)S(1)} %copy-done.8, s32[2,6]{1,0:T(2,128)S(1)} %copy-done.7, s32[2]{0:T(128)S(1)} %copy-done.9, s32[1,8]{1,0:T(1,128)S(1)} %copy-done.10, ...), custom_call_target="tpu_custom_call" | custom-call | tf_op jit(solution)/shard_map/pallas_call | solution.py:593
  98.6 0.8 multiply_subtract_fusion
  (1 shorter events, 0.0 us)
Async XLA Ops:
  0.6 1.1 %copy-start.1 = (bf16[8,64,128]{2,1,0:T(8,128)(2,1)S(1)}, bf16[8,64,128]{2,1,0:T(8,128)(2,1)}, u32[]{:S(2)}) copy-start(bf16[8,64,128]{2,1,0:T(8,128)(2,1)} %rhs.1) | copy-start | bytes 393220
  0.6 1.1 %copy-start.3 = (f32[1,64,64]{2,1,0:T(8,128)S(1)}, f32[1,64,64]{2,1,0:T(8,128)}, u32[]{:S(2)}) copy-start(f32[1,64,64]{2,1,0:T(8,128)} %param.23) | copy-start | bytes 49156
  0.7 1.1 %copy-start.4 = (f32[2,8,56]{2,1,0:T(8,128)S(1)}, f32[2,8,56]{2,1,0:T(8,128)}, u32[]{:S(2)}) copy-start(f32[2,8,56]{2,1,0:T(8,128)} %coarse_blocks.1) | copy-start | bytes 10756
  0.7 1.1 %copy-start.5 = (f32[2,8,8]{2,1,0:T(8,128)S(1)}, f32[2,8,8]{2,1,0:T(8,128)}, u32[]{:S(2)}) copy-start(f32[2,8,8]{2,1,0:T(8,128)} %coarse_inverses.1) | copy-start | bytes 1540
  0.7 1.1 %copy-start.6 = (s32[8,6]{1,0:T(8,128)S(1)}, s32[8,6]{1,0:T(8,128)}, u32[]{:S(2)}) copy-start(s32[8,6]{1,0:T(8,128)} %table.1) | copy-start | bytes 580
  0.7 1.1 %copy-start.7 = (s32[2,6]{1,0:T(2,128)S(1)}, s32[2,6]{1,0:T(2,128)}, u32[]{:S(2)}) copy-start(s32[2,6]{1,0:T(2,128)} %coarse_table.1) | copy-start | bytes 148
  0.7 1.1 %copy-start.8 = (s32[8]{0:T(128)S(1)}, s32[8]{0:T(128)}, u32[]{:S(2)}) copy-start(s32[8]{0:T(128)} %member.1) | copy-start | bytes 100
  0.7 1.1 %copy-start.9 = (s32[2]{0:T(128)S(1)}, s32[2]{0:T(128)}, u32[]{:S(2)}) copy-start(s32[2]{0:T(128)} %coarse_map.1) | copy-start | bytes 28
  0.7 1.1 %copy-start.10 = (s32[1,8]{1,0:T(1,128)S(1)}, s32[1,8]{1,0:T(1,128)}, u32[]{:S(2)}) copy-start(s32[1,8]{1,0:T(1,128)} %owner.1) | copy-start | bytes 100
  1.8 1.2 %copy-start = (f32[8,64,448]{2,1,0:T(8,128)S(1)}, f32[8,64,448]{2,1,0:T(8,128)}, u32[]{:S(2)}) copy-start(f32[8,64,448]{2,1,0:T(8,128)} %blocks.1) | copy-start | bytes 2752516
  3.0 0.9 copy-start.2

commit v2 on v1

v2 whole, which is shorter than its diff:
```python
import functools

import jax
import jax.numpy as jnp
from jax import lax
from jax.experimental import pallas as pl
from jax.experimental.pallas import tpu as pltpu
from jax.sharding import PartitionSpec as P

OMEGA = 0.7
LOW_BOUND = 0.25
UPPER_LIMIT = 1.9
THETA = (UPPER_LIMIT + LOW_BOUND) / 2.0
DELTA = (UPPER_LIMIT - LOW_BOUND) / 2.0
SIGMA = THETA / DELTA
RHO = [1.0 / SIGMA]
for _ in range(2):
    RHO.append(1.0 / (2.0 * SIGMA - RHO[-1]))
KEEP = [0.0, RHO[1] * RHO[0], RHO[2] * RHO[1]]
TAKE = [1.0 / THETA, 2.0 * RHO[1] / DELTA, 2.0 * RHO[2] / DELTA]

ELEMS = 8
NODES = 64
MODES = 8
SIDE = 3
LOADS = 128
HALO = 4
REACH = 3
SPAN = 2 * REACH + 1
MESH = pl.DeviceIdType.MESH
HIGHEST = lax.Precision.HIGHEST
F32 = jnp.float32
BF16 = jnp.bfloat16


def dot(a, b):
    return jnp.dot(a, b, preferred_element_type=F32)


def exact(a, b):
    return jnp.dot(a, b, preferred_element_type=F32, precision=HIGHEST)


def three(v):
    high = v.astype(BF16)
    rest = v - high.astype(F32)
    middle = rest.astype(BF16)
    low = (rest - middle.astype(F32)).astype(BF16)
    return high, middle, low


def iota(shape, dim):
    return lax.broadcasted_iota(jnp.int32, shape, dim)


def kernel(
    sizes,
    table,
    member,
    coarse_table,
    coarse_map,
    owner,
    rhs_hbm,
    inverses_hbm,
    blocks_hbm,
    basis_hbm,
    coarse_blocks,
    coarse_inverses,
    group_inverse,
    x_out,
    applied_out,
    step_out,
    rhs,
    inverses,
    blocks,
    basis,
    near,
    far,
    give,
    edge,
    da,
    a,
    window,
    halo,
    window_m,
    halo_m,
    update,
    direction,
    answer,
    acc,
    field,
    sent,
    landed,
    prolong,
    prolong_t,
    m_one,
    m_two,
    m_three,
    m_sent,
    m_landed,
    strip_sent,
    strip_landed,
    share_sent,
    share_landed,
    pack,
    packs,
    kmat,
    amat,
    cmat,
    dmat,
    left,
    strip,
    own_b,
    all_b,
    part,
    parts_near,
    total,
    parts_far,
    load_sem,
    send_sem,
    recv_sem,
    m_send,
    m_recv,
    strip_send,
    strip_recv,
    share_send,
    share_recv,
    pack_send,
    pack_recv,
    b_send,
    b_recv,
    sum_send,
    sum_recv,
):
    ngx, ngy, ngrp = sizes
    groups = ngx * ngy
    devices = groups * ngrp
    wide = SPAN * ngrp * 16
    full = kmat.shape[0]
    rem, div = lax.rem, lax.div
    gx, gy, grp = (lax.axis_index(name) for name in ("gx", "gy", "grp"))
    group = gx * ngy + gy
    me = group * ngrp + grp

    def place(index):
        return (div(index, ngy * ngrp), rem(div(index, ngrp), ngy), rem(index, ngrp))

    before = place(rem(me + devices - 1, devices))
    after = place(rem(me + 1, devices))

    def gather_partner(i):
        turn = div(i, ngrp)
        half = div(turn + 1, 2)
        offset = half * (1 - 2 * rem(turn, 2))
        to_group = rem(group + offset + groups, groups)
        slot = (REACH - offset) * ngrp + grp
        return (div(to_group, ngy), rem(to_group, ngy), rem(grp + i, ngrp)), slot

    near_count = ngx * ngrp
    near_rank = gx * ngrp + grp

    def near_partner(i):
        rank = rem(near_rank + rem(near_count // 2 - 2 + i, near_count - 1) + 1, near_count)
        return (div(rank, ngrp), gy, rem(rank, ngrp))

    def far_partner(i):
        half = div(i, 2)
        return (gx, rem(gy + ngy // 2 + half * (2 * rem(i, 2) - 1) + ngy, ngy), grp)

    barrier = pltpu.get_barrier_semaphore()

    def greet(partner, count):
        def body(i, carry):
            pl.semaphore_signal(barrier, inc=1, device_id=partner(i), device_id_type=MESH)
            return carry

        lax.fori_loop(1, count, body, 0)

    greet(lambda i: gather_partner(i)[0], SPAN * ngrp)

    loads = []
    for i, (source, target) in enumerate(
        ((rhs_hbm, rhs), (inverses_hbm, inverses), (blocks_hbm, blocks), (basis_hbm, basis))
    ):
        copy = pltpu.make_async_copy(source, target, load_sem.at[i])
        copy.start()
        loads.append(copy)
    greet(near_partner, near_count)
    greet(far_partner, ngy)
    greetings = (SPAN * ngrp - 1) + (near_count - 1) + (ngy - 1)

    for side in range(2):
        chosen = [jnp.int32(0) for _ in range(HALO)]
        count = jnp.int32(0)
        for e in range(ELEMS):
            t = table[e, side]
            flag = (t >= 0) & (t < ELEMS) if side == 0 else t >= 2 * ELEMS
            chosen = [jnp.where(flag & (count == j), e, chosen[j]) for j in range(HALO)]
            count += flag.astype(jnp.int32)
        for j in range(HALO):
            give[side, j] = chosen[j]

    loads[0].wait()
    loads[1].wait()
    for e in range(ELEMS):
        pieces = jnp.concatenate(three(inverses[e]), axis=0)
        o = dot(pieces, rhs[e])
        q = o[0:64] + (o[64:128] + o[128:192])
        update[e] = q
        d = q * TAKE[0]
        direction[e] = d
        answer[e] = d

    pl.semaphore_wait(barrier, greetings)

    def ring(source, target, send, recv, side):
        return pltpu.make_async_remote_copy(
            src_ref=source,
            dst_ref=target,
            send_sem=send,
            recv_sem=recv,
            device_id=before if side == 0 else after,
            device_id_type=MESH,
        )

    pending = []

    def both(k, source, target, send, recv):
        copies = [ring(source.at[k, s], target.at[k, 1 - s], send.at[k, s], recv.at[k, s], s) for s in range(2)]
        for copy in copies:
            copy.start()
        pending.extend(copies)
        return copies

    def arrive(copies):
        for copy in copies:
            copy.wait_recv()

    def exchange(k, source):
        for side in range(2):
            for j in range(HALO):
                sent[k, side, j] = source[give[side, j]]
        return both(k, sent, landed, send_sem, recv_sem)

    def exchange_m(k, source):
        for side in range(2):
            for j in range(HALO):
                m_sent[k, side, j] = pltpu.roll(source[give[side, j]], 16 if side == 0 else LOADS - 16, 1)
        return both(k, m_sent, m_landed, m_send, m_recv)

    def store_pieces(ref, slot, value):
        high, middle, low = three(value)
        ref[slot, :, 0:128] = high
        ref[slot, :, 128:256] = middle
        ref[slot, :, 256:384] = low

    def cut(source, into):
        for e in range(ELEMS):
            store_pieces(into, e, source[e])

    def cut_halo(source, k, into):
        for side in range(2):
            for j in range(HALO):
                store_pieces(into, side * HALO + j, source[k, side, j])

    def products(matrix, stack):
        o = dot(matrix, stack[:, 0:256])
        p = dot(matrix[0:64], stack[:, 256:384])
        small = o[64:128, 128:256] + o[128:192, 0:128] + p
        return o[0:64, 0:128] + ((o[0:64, 128:256] + o[64:128, 0:128]) + small)

    def local_part(matrix, e, of):
        stack = jnp.concatenate([of[e]] + [of[near[e, k]] for k in range(6)], axis=0)
        return products(matrix[e], stack)

    def halo_part(matrix, e, of):
        stack = jnp.concatenate([of[far[e, 0]], of[far[e, 1]]], axis=0)
        return products(matrix[e, :, 64:192], stack)

    def gather(source, target, send, recv):
        own_slot = REACH * ngrp + grp

        def body(i, carry):
            device, slot = gather_partner(SPAN * ngrp - i)
            pltpu.make_async_remote_copy(
                src_ref=source,
                dst_ref=target.at[slot],
                send_sem=send,
                recv_sem=recv,
                device_id=device,
                device_id_type=MESH,
            ).start()
            return carry

        lax.fori_loop(1, SPAN * ngrp, body, 0)
        target[own_slot] = source[...]

    def wait_bytes(target, count, sem):
        pltpu.make_async_copy(target.at[pl.ds(0, count)], target.at[pl.ds(0, count)], sem).wait()

    gathered = SPAN * ngrp - 1

    copies = exchange(0, direction)

    loads[3].wait()
    first_lane = 16 * SIDE
    for e in range(ELEMS):
        spot = iota((16, MODES), 0) == iota((16, MODES), 1) + MODES * member[e]
        rows = exact(spot.astype(F32), basis[e])
        prolong_t[e] = rows
        tall = jnp.concatenate(
            [jnp.zeros((first_lane, NODES), F32), rows, jnp.zeros((112 - first_lane, NODES), F32)], axis=0
        )
        prolong[e] = tall.T
    copies_m = [exchange_m(0, prolong)]

    lanes = iota((8, 128), 1)
    for agg in range(2):
        row = iota((56, 128), 0)
        want = jnp.full((56, 128), 2 + agg, jnp.int32)
        for k in range(6):
            want = jnp.where(row // 8 == k + 1, coarse_table[agg, k], want)
        spot = iota((56, 128), 1) == want * 8 + row % 8
        t_rows = exact(coarse_blocks[agg], spot.astype(F32))
        small = iota((8, 128), 1) == iota((8, 128), 0) + 48 + 8 * agg
        d_rows = exact(coarse_inverses[agg], small.astype(F32))
        whole = coarse_map[agg]
        coarse_rows = group_inverse[whole]
        mine = owner[0, whole]
        kept = jnp.zeros((8, 64), F32)
        for c in range(8):
            same = (owner[0, c] == mine).astype(F32)
            kept = jnp.where(iota((8, 64), 1) // 8 == c, same, kept)
        shift = iota((64, 128), 1) == iota((64, 128), 0) + 64
        m_rows = exact(jnp.where(kept > 0.5, coarse_rows, 0.0), shift.astype(F32))
        s_rows = (lanes == iota((8, 128), 0) + 8 * whole).astype(F32)
        dt_rows = pltpu.roll(exact(coarse_inverses[agg], t_rows), 64, 1)
        first = jnp.where(lanes < 48, t_rows, jnp.where(lanes < 64, d_rows, m_rows))
        pack[8 * agg : 8 * agg + 8, 0:128] = first
        pack[8 * agg : 8 * agg + 8, 128:256] = jnp.where(lanes < 64, s_rows, dt_rows)
    gather(pack, packs, pack_send, pack_recv)

    for e in range(ELEMS):
        for k in range(6):
            t = table[e, k]
            here = (t >= ELEMS) & (t < 2 * ELEMS)
            near[e, k] = jnp.where(here, t - ELEMS, ELEMS)
    for side in range(2):
        chosen = [jnp.int32(0) for _ in range(HALO)]
        count = jnp.int32(0)
        for e in range(ELEMS):
            t = table[e, side]
            rank = jnp.int32(0)
            for other in range(ELEMS):
                u = table[other, side]
                lower = (u >= 0) & (u < t) if side == 0 else (u >= 2 * ELEMS) & (u < t)
                rank += lower.astype(jnp.int32)
            named = (t >= 0) & (t < ELEMS) if side == 0 else t >= 2 * ELEMS
            rank = jnp.minimum(rank, HALO - 1)
            far[e, side] = jnp.where(named, side * HALO + rank, 2 * HALO)
            chosen = [jnp.where(named & (rank == j), e, chosen[j]) for j in range(HALO)]
            count += named.astype(jnp.int32)
        for j in range(HALO):
            edge[side, j] = chosen[j]
        edge[side, HALO] = count
    window[ELEMS] = jnp.zeros((NODES, 3 * LOADS), BF16)
    window_m[ELEMS] = jnp.zeros((NODES, 3 * LOADS), BF16)
    halo[2 * HALO] = jnp.zeros((NODES, 3 * LOADS), BF16)
    halo_m[2 * HALO] = jnp.zeros((NODES, 3 * LOADS), BF16)

    loads[2].wait()
    for e in range(ELEMS):
        high, middle, low = three(exact(inverses[e], blocks[e]))
        da[e, 0:64] = high
        da[e, 64:128] = middle
        da[e, 128:192] = low

    def finish_step(k, copies, matrix, finish):
        arrive(copies)
        cut_halo(landed, k, halo)
        for e in range(ELEMS):
            finish(e, acc[e] + halo_part(matrix, e, halo))

    def local_step(matrix, source):
        cut(source, window)
        for e in range(ELEMS):
            acc[e] = local_part(matrix, e, window)

    def next_m(k, source, target):
        arrive(copies_m[k])
        cut(source, window_m)
        cut_halo(m_landed, k, halo_m)
        for e in range(ELEMS):
            target[e] = local_part(da, e, window_m) + halo_part(da, e, halo_m)

    def pre_finish(i):
        def finish(e, value):
            q = update[e] - value
            update[e] = q
            if i < 3:
                d = KEEP[i] * direction[e] + TAKE[i] * q
                direction[e] = d
                answer[e] = answer[e] + d
            else:
                field[e] = answer[e] + OMEGA * q

        return finish

    local_step(da, direction)
    for e in range(ELEMS):
        high, middle, low = three(blocks[e])
        a[e, 0:64] = high
        a[e, 64:128] = middle
        a[e, 128:192] = low
    for side in range(2):
        column = slice(64 + 64 * side, 128 + 64 * side)
        pieces = []
        for j in range(HALO):
            e = edge[side, j]
            rows = exact(prolong_t[e], blocks[e, :, column])
            pieces.append(jnp.where(edge[side, HALO] > j, rows, 0.0))
        strip_sent[0, side] = jnp.concatenate(pieces, axis=1)
    strip_copies = both(0, strip_sent, strip_landed, strip_send, strip_recv)
    finish_step(0, copies, da, pre_finish(1))

    copies = exchange(1, direction)
    next_m(0, prolong, m_one)
    copies_m.append(exchange_m(1, m_one))
    local_step(da, direction)

    wait_bytes(packs, gathered, pack_recv)
    wait_bytes(packs, gathered, pack_send)
    for ref in (kmat, amat, cmat, dmat):
        ref[...] = jnp.zeros((full, full), F32)
    blank = jnp.zeros((16, full - 128), F32)

    def spread(rows, first, count, move):
        keep = (iota((16, 128), 1) >= first) & (iota((16, 128), 1) < first + count)
        rows = jnp.concatenate([jnp.where(keep, rows, 0.0), blank], axis=1)
        return pltpu.roll(rows, (move - first) % full, 1)

    for w in range(SPAN * ngrp):
        one = packs[w, :, 0:128]
        two = packs[w, :, 128:256]
        here = slice(16 * w, 16 * w + 16)
        amat[here, :] = spread(one, 0, 48, 16 * (w - 1))
        dmat[here, :] = spread(one, 48, 16, 16 * w)
        kmat[here, :] = spread(two, 64, 48, 16 * (w - 1))
    for s in range(SPAN):
        parts = [packs[s * ngrp + j] for j in range(ngrp)]
        stacked = jnp.concatenate(parts, axis=0)
        coarse = stacked[:, 64:128]
        places = stacked[:, 128:192]
        block = lax.dot_general(
            coarse, places, (((1,), (1,)), ((), ())), preferred_element_type=F32, precision=HIGHEST
        )
        size = 16 * ngrp
        row = jnp.concatenate([block, jnp.zeros((size, full - size), F32)], axis=1)
        cmat[size * s : size * s + size, :] = pltpu.roll(row, size * s, 1) if s else row
    finish_step(1, copies, da, pre_finish(2))

    copies = exchange(2, direction)
    next_m(1, m_one, m_two)
    copies_m.append(exchange_m(2, m_two))
    local_step(da, direction)

    def smooth(rows):
        q = rows
        d = rows * TAKE[0]
        y = d
        for i in (1, 2):
            q = q - exact(d, kmat[...])
            d = KEEP[i] * d + TAKE[i] * q
            y = y + d
        return y

    held = 16 * (2 * SIDE + 1)
    start = (REACH * ngrp + grp - SIDE) * 16
    unit = (iota((128, full), 1) == iota((128, full), 0) + start) & (iota((128, full), 0) < held)
    unit = unit.astype(F32)
    u = smooth(unit)
    v = exact(u, kmat[...])
    strip[...] = v
    left[...] = 2.0 * u
    finish_step(2, copies, da, pre_finish(3))

    arrive(strip_copies)
    for side in range(2):
        edge_rows = jnp.concatenate([field[give[side, j]] for j in range(HALO)], axis=0)
        share_sent[0, side] = exact(strip_landed[0, side], edge_rows)
    share_copies = both(0, share_sent, share_landed, share_send, share_recv)
    copies = exchange(3, update)
    cut(field, window)
    mine_b = jnp.zeros((16, LOADS), F32)
    for e in range(ELEMS):
        acc[e] = rhs[e].astype(F32) - local_part(a, e, window)
    for e in range(ELEMS):
        mine_b = mine_b + exact(prolong_t[e], acc[e])
    next_m(2, m_two, m_three)
    local_step(da, update)
    arrive(share_copies)
    own_b[...] = mine_b - (share_landed[0, 0] + share_landed[0, 1])
    gather(own_b, all_b, b_send, b_recv)

    unit = (iota((128, full), 1) == iota((128, full), 0) + start) & (iota((128, full), 0) < held)
    m = exact(unit.astype(F32) - strip[...], cmat[...])
    y = smooth(strip[...] + exact(m, amat[...]))
    strip[...] = m + exact(left[...] - y, dmat[...])

    def post_first(e, value):
        q0 = update[e]
        d0 = TAKE[0] * q0
        q1 = q0 - TAKE[0] * value
        d1 = KEEP[1] * d0 + TAKE[1] * q1
        update[e] = q1
        direction[e] = d1
        answer[e] = answer[e] + d0 + d1

    finish_step(3, copies, da, post_first)

    for e in range(ELEMS):
        one, two = m_one[e], m_two[e]
        g = one - OMEGA * two
        h = g - TAKE[0] * (two - OMEGA * m_three[e])
        step = KEEP[1] * TAKE[0] * g + TAKE[1] * h
        whole = (prolong[e] - OMEGA * one) - TAKE[0] * g - step
        m_one[e] = step
        m_two[e] = h
        m_three[e] = whole

    wait_bytes(all_b, gathered, b_recv)
    values = all_b[...].reshape(wide, LOADS)
    padded = jnp.concatenate([values, jnp.zeros((full - wide, LOADS), F32)], axis=0)
    c = exact(strip[...], padded)
    rows = ELEMS * NODES
    change = exact(m_one[...].reshape(rows, LOADS), c).reshape(ELEMS, NODES, LOADS)
    direction[...] = direction[...] - change

    copies = exchange(4, direction)
    change = exact(m_two[...].reshape(rows, LOADS), c).reshape(ELEMS, NODES, LOADS)
    update[...] = update[...] - change
    change = exact(m_three[...].reshape(rows, LOADS), c).reshape(ELEMS, NODES, LOADS)
    answer[...] = answer[...] + change
    local_step(da, direction)
    wait_bytes(all_b, gathered, b_send)

    def post_last(e, value):
        q = update[e] - value
        answer[e] = answer[e] + (KEEP[2] * direction[e] + TAKE[2] * q)

    finish_step(4, copies, da, post_last)

    copies = exchange(5, answer)
    local_step(a, answer)
    sums = [jnp.zeros((8, LOADS), F32), jnp.zeros((8, LOADS), F32)]
    for e in range(ELEMS):
        x = answer[e]
        x_out[e] = x
        sums[0] = sums[0] + jnp.sum((rhs[e].astype(F32) * x).reshape(8, 8, LOADS), axis=0)

    def last(e, value):
        applied_out[e] = value
        sums[1] = sums[1] + jnp.sum((answer[e] * value).reshape(8, 8, LOADS), axis=0)

    finish_step(5, copies, a, last)
    row = iota((8, LOADS), 0)
    numerator = jnp.sum(sums[0], axis=0, keepdims=True)
    denominator = jnp.sum(sums[1], axis=0, keepdims=True)
    part[...] = jnp.where(row == 0, numerator, jnp.where(row == 1, denominator, 0.0))

    def combine(source, target, partner, rank, count, which):
        def body(i, carry):
            pltpu.make_async_remote_copy(
                src_ref=source,
                dst_ref=target.at[rank],
                send_sem=sum_send.at[which],
                recv_sem=sum_recv.at[which],
                device_id=partner(i),
                device_id_type=MESH,
            ).start()
            return carry

        lax.fori_loop(1, count, body, 0)
        target[rank] = source[...]
        wait_bytes(target, count - 1, sum_recv.at[which])
        return jnp.sum(target[...], axis=0)

    total[...] = combine(part, parts_near, near_partner, near_rank, near_count, 0)
    whole = combine(total, parts_far, far_partner, gy, ngy, 1)
    step_out[...] = jnp.broadcast_to(whole[0:1] / whole[1:2], (8, LOADS))
    wait_bytes(parts_near, near_count - 1, sum_send.at[0])
    wait_bytes(parts_far, ngy - 1, sum_send.at[1])
    for copy in pending:
        copy.wait_send()


def on_device(
    sizes,
    rhs,
    element_blocks,
    element_table,
    element_block_inverses,
    basis,
    element_aggregate,
    aggregate_blocks,
    aggregate_table,
    aggregate_inverse,
    coarse_map,
    coarse_owner,
    coarse_inverse,
):
    ngx, ngy, ngrp = sizes
    held = SPAN * ngrp
    full = -(-held * 16 // 128) * 128
    smem = pl.BlockSpec(memory_space=pltpu.SMEM)
    vmem = pl.BlockSpec(memory_space=pltpu.VMEM)
    hbm = pl.BlockSpec(memory_space=pltpu.HBM)
    shape = (ELEMS, NODES, LOADS)
    exchanges = 6
    cut_shape = (ELEMS + 1, NODES, 3 * LOADS)
    scratch = [
        pltpu.VMEM(shape, BF16),
        pltpu.VMEM((ELEMS, NODES, NODES), F32),
        pltpu.VMEM((ELEMS, NODES, 7 * NODES), F32),
        pltpu.VMEM((ELEMS, MODES, NODES), F32),
        pltpu.SMEM((ELEMS, 6), jnp.int32),
        pltpu.SMEM((ELEMS, 2), jnp.int32),
        pltpu.SMEM((2, HALO), jnp.int32),
        pltpu.SMEM((2, HALO + 1), jnp.int32),
        pltpu.VMEM((ELEMS, 192, 448), BF16),
        pltpu.VMEM((ELEMS, 192, 448), BF16),
        *([pltpu.VMEM(cut_shape, BF16)] * 4),
        *([pltpu.VMEM(shape, F32)] * 5),
        *([pltpu.VMEM((exchanges, 2, HALO, NODES, LOADS), F32)] * 2),
        pltpu.VMEM(shape, F32),
        pltpu.VMEM((ELEMS, 16, NODES), F32),
        *([pltpu.VMEM(shape, F32)] * 3),
        *([pltpu.VMEM((3, 2, HALO, NODES, LOADS), F32)] * 2),
        *([pltpu.VMEM((1, 2, 16, HALO * NODES), F32)] * 2),
        *([pltpu.VMEM((1, 2, 16, LOADS), F32)] * 2),
        pltpu.VMEM((16, 256), F32),
        pltpu.VMEM((held, 16, 256), F32),
        *([pltpu.VMEM((full, full), F32)] * 4),
        *([pltpu.VMEM((128, full), F32)] * 2),
        pltpu.VMEM((16, LOADS), F32),
        pltpu.VMEM((held, 16, LOADS), F32),
        pltpu.VMEM((8, LOADS), F32),
        pltpu.VMEM((ngx * ngrp, 8, LOADS), F32),
        pltpu.VMEM((8, LOADS), F32),
        pltpu.VMEM((ngy, 8, LOADS), F32),
        pltpu.SemaphoreType.DMA((4,)),
        *([pltpu.SemaphoreType.DMA((exchanges, 2))] * 2),
        *([pltpu.SemaphoreType.DMA((3, 2))] * 2),
        *([pltpu.SemaphoreType.DMA((1, 2))] * 4),
        *([pltpu.SemaphoreType.DMA] * 4),
        *([pltpu.SemaphoreType.DMA((2,))] * 2),
    ]
    x, applied, step = pl.pallas_call(
        functools.partial(kernel, sizes),
        out_shape=(
            jax.ShapeDtypeStruct(shape, F32),
            jax.ShapeDtypeStruct(shape, F32),
            jax.ShapeDtypeStruct((8, LOADS), F32),
        ),
        in_specs=[smem] * 5 + [hbm] * 4 + [vmem] * 3,
        out_specs=(vmem, vmem, vmem),
        scratch_shapes=scratch,
        compiler_params=pltpu.CompilerParams(
            collective_id=0, has_side_effects=True, vmem_limit_bytes=48 * 1024 * 1024
        ),
    )(
        element_table,
        element_aggregate,
        aggregate_table,
        coarse_map,
        coarse_owner,
        rhs,
        element_block_inverses,
        element_blocks,
        jnp.swapaxes(basis, 1, 2),
        aggregate_blocks,
        aggregate_inverse,
        coarse_inverse.reshape(8, 8, 64),
    )
    step = step[0:1][None]
    return step * x, rhs.astype(F32) - step * applied


def solution(mesh):
    sizes = tuple(mesh.shape[name] for name in ("gx", "gy", "grp"))
    slabs = P(("gx", "gy", "grp"), None, None)
    pairs = P(("gx", "gy", "grp"), None)
    ids = P(("gx", "gy", "grp"))
    return jax.shard_map(
        functools.partial(on_device, sizes),
        mesh=mesh,
        in_specs=(
            slabs,
            slabs,
            pairs,
            slabs,
            slabs,
            ids,
            slabs,
            pairs,
            slabs,
            ids,
            P(("gx", "gy"), None),
            P(("gx", "gy"), None, None),
        ),
        out_specs=(slabs, slabs),
        check_vma=False,
    )
```

time: 99.7 us -> 94.9 us (0.952)
  Pallas kernels: 94.6 us -> 85.5 us
  local copies, waits for them, and re-layouts: 3.19 us -> 7.36 us
    pallas_call x1, Pallas kernels: 94.6 us -> 85.5 us  [on_device(): pl.pallas_call(functools.partial(kernel, sizes), out_shape=(jax.ShapeDtyp...]
    unnamed x23 -> x24, local copies, waits for them, and re-layouts: 3.19 us -> 7.35 us
where the time goes in v2:
time: 94.9 us; the launch traced here: 94.4 us
  Pallas kernels  85.5 us (90%)
  local copies, waits for them, and re-layouts  7.36 us (8%)
    pallas_call x1, Pallas kernels, on_device(): pl.pallas_call(functools.partial(kernel, sizes), out_shape=(jax.ShapeDtyp...  85.5 us
    unnamed x24, local copies, waits for them, and re-layouts  7.35 us

profile of v2, /device:TPU:1, one launch (start us, length us, event | category | flops | bytes accessed | tf_op | source)
XLA Modules:
  0.0 94.4 jit_solution(15263815343267726336)
XLA Ops:
  0.6 0.0 copy-start.10
  0.6 0.0 copy-start.11
  0.7 0.0 copy-start.8
  0.7 0.0 copy-start.9
  0.7 0.6 copy-done.10
  1.3 0.0 copy-done.11
  1.3 0.0 copy-done.8
  1.3 0.0 copy-done.9
  1.3 0.0 copy-start
  1.4 1.2 %copy-done = f32[8,64,448]{2,1,0:T(8,128)S(1)} copy-done((f32[8,64,448]{2,1,0:T(8,128)S(1)}, f32[8,64,448]{2,1,0:T(8,128)}, u32[]{:S(2)}) %copy-start) | copy-done | bytes 917528
  2.6 0.0 copy-start.1
  2.6 0.9 copy-done.1
  3.5 0.0 copy-start.2
  3.5 0.9 %copy-done.2 = f32[8,64,64]{2,1,0:T(8,128)S(1)} copy-done((f32[8,64,64]{2,1,0:T(8,128)S(1)}, f32[8,64,64]{2,1,0:T(8,128)}, u32[]{:S(2)}) %copy-start.2) | copy-done | bytes 131096
  4.4 0.0 copy-start.3
  4.4 0.8 copy-done.3
  5.2 0.0 copy-start.4
  5.2 0.8 copy-done.4
  5.9 0.0 copy-start.5
  5.9 0.7 copy-done.5
  6.6 0.0 copy-start.6
  6.6 0.7 copy-done.6
  7.3 0.0 copy-start.7
  7.3 0.7 copy-done.7
  8.0 85.5 %shard_map.131 = (f32[8,64,128]{2,1,0:T(8,128)S(1)}, f32[8,64,128]{2,1,0:T(8,128)S(1)}, f32[8,128]{1,0:T(8,128)S(1)}) custom-call(s32[8,6]{1,0:T(8,128)S(1)} %copy-done.7, s32[8]{0:T(128)S(1)} %copy-done.9, s32[2,6]{1,0:T(2,128)S(1)} %copy-done.8, s32[2]{0:T(128)S(1)} %copy-done.10, s32[1,8]{1,0:T(1,128)S(1)} %copy-done.11, ...), custom_call_target="tpu_custom_call" | custom-call | tf_op jit(solution)/shard_map/pallas_call | solution.py:658
  93.6 0.8 multiply_subtract_fusion
  (1 shorter events, 0.0 us)
Async XLA Ops:
  0.6 0.7 copy-start.10
  0.6 0.7 copy-start.11
  0.7 0.7 copy-start.8
  0.7 0.7 copy-start.9
  1.3 1.2 %copy-start = (f32[8,64,448]{2,1,0:T(8,128)S(1)}, f32[8,64,448]{2,1,0:T(8,128)}, u32[]{:S(2)}) copy-start(f32[8,64,448]{2,1,0:T(8,128)} %blocks_hbm.1) | copy-start | bytes 2752516
  2.6 0.9 copy-start.1
  3.5 0.9 %copy-start.2 = (f32[8,64,64]{2,1,0:T(8,128)S(1)}, f32[8,64,64]{2,1,0:T(8,128)}, u32[]{:S(2)}) copy-start(f32[8,64,64]{2,1,0:T(8,128)} %inverses_hbm.1) | copy-start | bytes 393220
  4.4 0.8 copy-start.3
  5.2 0.8 copy-start.4
  5.9 0.7 copy-start.5
  6.6 0.7 copy-start.6
  7.3 0.7 copy-start.7

commit v3 on v2

--- a/solution.py
+++ b/solution.py
@@ -243,10 +243,30 @@
         return both(k, sent, landed, send_sem, recv_sem)
 
     def exchange_m(k, source):
+        low, count = 16 * (SIDE - k), 16 * (2 * k + 1)
+        copies = []
         for side in range(2):
+            tall = jnp.concatenate([source[give[side, j]] for j in range(HALO)], axis=0)
+            m_sent[k, side, 0:count] = tall.T[low : low + count]
+            rows = pl.ds(0, count)
+            copy = ring(
+                m_sent.at[k, side, rows], m_landed.at[k, 1 - side, rows], m_send.at[k, side], m_recv.at[k, side], side
+            )
+            copy.start()
+            copies.append(copy)
+        pending.extend(copies)
+        return copies
+
+    def cut_halo_m(k):
+        low, count = 16 * (SIDE - k), 16 * (2 * k + 1)
+        for side in range(2):
+            first = low - 16 if side == 0 else low + 16
+            rows = [m_landed[k, side, 0:count], jnp.zeros((LOADS - first - count, HALO * NODES), F32)]
+            if first:
+                rows = [jnp.zeros((first, HALO * NODES), F32)] + rows
+            tall = jnp.concatenate(rows, axis=0).T
             for j in range(HALO):
-                m_sent[k, side, j] = pltpu.roll(source[give[side, j]], 16 if side == 0 else LOADS - 16, 1)
-        return both(k, m_sent, m_landed, m_send, m_recv)
+                store_pieces(halo_m, side * HALO + j, tall[NODES * j : NODES * j + NODES])
 
     def store_pieces(ref, slot, value):
         high, middle, low = three(value)
@@ -277,8 +297,7 @@
         stack = jnp.concatenate([of[far[e, 0]], of[far[e, 1]]], axis=0)
         return products(matrix[e, :, 64:192], stack)
 
-    def gather(source, target, send, recv):
-        own_slot = REACH * ngrp + grp
+    def gather(source, target, send, recv, first, stop):
 
         def body(i, carry):
             device, slot = gather_partner(SPAN * ngrp - i)
@@ -292,8 +311,7 @@
             ).start()
             return carry
 
-        lax.fori_loop(1, SPAN * ngrp, body, 0)
-        target[own_slot] = source[...]
+        lax.fori_loop(first, stop, body, 0)
 
     def wait_bytes(target, count, sem):
         pltpu.make_async_copy(target.at[pl.ds(0, count)], target.at[pl.ds(0, count)], sem).wait()
@@ -322,7 +340,7 @@
             want = jnp.where(row // 8 == k + 1, coarse_table[agg, k], want)
         spot = iota((56, 128), 1) == want * 8 + row % 8
         t_rows = exact(coarse_blocks[agg], spot.astype(F32))
-        small = iota((8, 128), 1) == iota((8, 128), 0) + 48 + 8 * agg
+        small = iota((8, 128), 1) == iota((8, 128), 0) + 48
         d_rows = exact(coarse_inverses[agg], small.astype(F32))
         whole = coarse_map[agg]
         coarse_rows = group_inverse[whole]
@@ -333,12 +351,12 @@
             kept = jnp.where(iota((8, 64), 1) // 8 == c, same, kept)
         shift = iota((64, 128), 1) == iota((64, 128), 0) + 64
         m_rows = exact(jnp.where(kept > 0.5, coarse_rows, 0.0), shift.astype(F32))
-        s_rows = (lanes == iota((8, 128), 0) + 8 * whole).astype(F32)
-        dt_rows = pltpu.roll(exact(coarse_inverses[agg], t_rows), 64, 1)
-        first = jnp.where(lanes < 48, t_rows, jnp.where(lanes < 64, d_rows, m_rows))
-        pack[8 * agg : 8 * agg + 8, 0:128] = first
-        pack[8 * agg : 8 * agg + 8, 128:256] = jnp.where(lanes < 64, s_rows, dt_rows)
-    gather(pack, packs, pack_send, pack_recv)
+        place_rows = jnp.where(lanes == 56, whole.astype(F32), m_rows)
+        first = jnp.where(lanes < 48, t_rows, jnp.where(lanes < 56, d_rows, place_rows))
+        pack[8 * agg : 8 * agg + 8] = first
+    half_way = SPAN * ngrp // 2
+    packs[REACH * ngrp + grp] = pack[...]
+    gather(pack, packs, pack_send, pack_recv, 1, half_way)
 
     for e in range(ELEMS):
         for k in range(6):
@@ -389,7 +407,7 @@
     def next_m(k, source, target):
         arrive(copies_m[k])
         cut(source, window_m)
-        cut_halo(m_landed, k, halo_m)
+        cut_halo_m(k)
         for e in range(ELEMS):
             target[e] = local_part(da, e, window_m) + halo_part(da, e, halo_m)
 
@@ -426,44 +444,63 @@
     copies = exchange(1, direction)
     next_m(0, prolong, m_one)
     copies_m.append(exchange_m(1, m_one))
+    gather(pack, packs, pack_send, pack_recv, half_way, SPAN * ngrp)
+    local_step(da, direction)
+
+    finish_step(1, copies, da, pre_finish(2))
+
+    copies = exchange(2, direction)
+    next_m(1, m_one, m_two)
+    copies_m.append(exchange_m(2, m_two))
     local_step(da, direction)
 
     wait_bytes(packs, gathered, pack_recv)
     wait_bytes(packs, gathered, pack_send)
     for ref in (kmat, amat, cmat, dmat):
         ref[...] = jnp.zeros((full, full), F32)
-    blank = jnp.zeros((16, full - 128), F32)
 
     def spread(rows, first, count, move):
-        keep = (iota((16, 128), 1) >= first) & (iota((16, 128), 1) < first + count)
-        rows = jnp.concatenate([jnp.where(keep, rows, 0.0), blank], axis=1)
+        lane = iota(rows.shape, 1)
+        rows = jnp.where((lane >= first) & (lane < first + count), rows, 0.0)
+        rows = jnp.concatenate([rows, jnp.zeros((rows.shape[0], full - 128), F32)], axis=1)
         return pltpu.roll(rows, (move - first) % full, 1)
 
     for w in range(SPAN * ngrp):
-        one = packs[w, :, 0:128]
-        two = packs[w, :, 128:256]
-        here = slice(16 * w, 16 * w + 16)
-        amat[here, :] = spread(one, 0, 48, 16 * (w - 1))
-        dmat[here, :] = spread(one, 48, 16, 16 * w)
-        kmat[here, :] = spread(two, 64, 48, 16 * (w - 1))
+        one = packs[w]
+        amat[16 * w : 16 * w + 16, :] = spread(one, 0, 48, 16 * (w - 1))
+        for agg in range(2):
+            at = 16 * w + 8 * agg
+            dmat[at : at + 8, :] = spread(one[8 * agg : 8 * agg + 8], 48, 8, at)
+    tall = packs[...].reshape(wide, 128)
+    tall = jnp.where(iota((wide, 128), 1) < 48, tall, 0.0)
+    tall = exact(dmat[...], jnp.concatenate([tall, jnp.zeros((full - wide, 128), F32)], axis=0))
+    for w in range(SPAN * ngrp):
+        kmat[16 * w : 16 * w + 16, :] = spread(tall[16 * w : 16 * w + 16], 0, 48, 16 * (w - 1))
+    size = 16 * ngrp
     for s in range(SPAN):
-        parts = [packs[s * ngrp + j] for j in range(ngrp)]
-        stacked = jnp.concatenate(parts, axis=0)
+        stacked = jnp.concatenate([packs[s * ngrp + j] for j in range(ngrp)], axis=0)
         coarse = stacked[:, 64:128]
-        places = stacked[:, 128:192]
+        target = 8.0 * stacked[:, 56:57] + (iota((size, 64), 0) % 8).astype(F32)
+        places = jnp.where(jnp.abs(iota((size, 64), 1).astype(F32) - target) < 0.5, 1.0, 0.0)
         block = lax.dot_general(
             coarse, places, (((1,), (1,)), ((), ())), preferred_element_type=F32, precision=HIGHEST
         )
-        size = 16 * ngrp
         row = jnp.concatenate([block, jnp.zeros((size, full - size), F32)], axis=1)
         cmat[size * s : size * s + size, :] = pltpu.roll(row, size * s, 1) if s else row
-    finish_step(1, copies, da, pre_finish(2))
-
-    copies = exchange(2, direction)
-    next_m(1, m_one, m_two)
-    copies_m.append(exchange_m(2, m_two))
-    local_step(da, direction)
-
+    finish_step(2, copies, da, pre_finish(3))
+
+    arrive(strip_copies)
+    for side in range(2):
+        edge_rows = jnp.concatenate([field[give[side, j]] for j in range(HALO)], axis=0)
+        share_sent[0, side] = exact(strip_landed[0, side], edge_rows)
+    share_copies = both(0, share_sent, share_landed, share_send, share_recv)
+    copies = exchange(3, update)
+    cut(field, window)
+    mine_b = jnp.zeros((16, LOADS), F32)
+    for e in range(ELEMS):
+        acc[e] = rhs[e].astype(F32) - local_part(a, e, window)
+    for e in range(ELEMS):
+        mine_b = mine_b + exact(prolong_t[e], acc[e])
     def smooth(rows):
         q = rows
         d = rows * TAKE[0]
@@ -482,26 +519,14 @@
     v = exact(u, kmat[...])
     strip[...] = v
     left[...] = 2.0 * u
-    finish_step(2, copies, da, pre_finish(3))
-
-    arrive(strip_copies)
-    for side in range(2):
-        edge_rows = jnp.concatenate([field[give[side, j]] for j in range(HALO)], axis=0)
-        share_sent[0, side] = exact(strip_landed[0, side], edge_rows)
-    share_copies = both(0, share_sent, share_landed, share_send, share_recv)
-    copies = exchange(3, update)
-    cut(field, window)
-    mine_b = jnp.zeros((16, LOADS), F32)
-    for e in range(ELEMS):
-        acc[e] = rhs[e].astype(F32) - local_part(a, e, window)
-    for e in range(ELEMS):
-        mine_b = mine_b + exact(prolong_t[e], acc[e])
+
     next_m(2, m_two, m_three)
-    local_step(da, update)
     arrive(share_copies)
     own_b[...] = mine_b - (share_landed[0, 0] + share_landed[0, 1])
-    gather(own_b, all_b, b_send, b_recv)
-
+    gather(own_b, all_b, b_send, b_recv, 1, SPAN * ngrp)
+    all_b[REACH * ngrp + grp] = own_b[...]
+
+    local_step(da, update)
     unit = (iota((128, full), 1) == iota((128, full), 0) + start) & (iota((128, full), 0) < held)
     m = exact(unit.astype(F32) - strip[...], cmat[...])
     y = smooth(strip[...] + exact(m, amat[...]))
@@ -635,11 +660,11 @@
         pltpu.VMEM(shape, F32),
         pltpu.VMEM((ELEMS, 16, NODES), F32),
         *([pltpu.VMEM(shape, F32)] * 3),
-        *([pltpu.VMEM((3, 2, HALO, NODES, LOADS), F32)] * 2),
+        *([pltpu.VMEM((3, 2, 16 * (2 * SIDE - 1), HALO * NODES), F32)] * 2),
         *([pltpu.VMEM((1, 2, 16, HALO * NODES), F32)] * 2),
         *([pltpu.VMEM((1, 2, 16, LOADS), F32)] * 2),
-        pltpu.VMEM((16, 256), F32),
-        pltpu.VMEM((held, 16, 256), F32),
+        pltpu.VMEM((16, LOADS), F32),
+        pltpu.VMEM((held, 16, LOADS), F32),
         *([pltpu.VMEM((full, full), F32)] * 4),
         *([pltpu.VMEM((128, full), F32)] * 2),
         pltpu.VMEM((16, LOADS), F32),

time: 94.9 us -> 87.1 us (0.918)
  Pallas kernels: 85.5 us -> 77.8 us
    pallas_call x1, Pallas kernels: 85.5 us -> 77.8 us  [on_device(): pl.pallas_call(functools.partial(kernel, sizes), out_shape=(jax.ShapeDtyp...]
where the time goes in v3:
time: 87.1 us; the launch traced here: 86.7 us
  Pallas kernels  77.8 us (89%)
  local copies, waits for them, and re-layouts  7.36 us (8%)
    pallas_call x1, Pallas kernels, on_device(): pl.pallas_call(functools.partial(kernel, sizes), out_shape=(jax.ShapeDtyp...  77.8 us
    unnamed x24, local copies, waits for them, and re-layouts  7.35 us

profile of v3, /device:TPU:1, one launch (start us, length us, event | category | flops | bytes accessed | tf_op | source)
XLA Modules:
  0.0 86.7 jit_solution(2806447067424278932)
XLA Ops:
  0.6 0.0 copy-start.10
  0.6 0.0 copy-start.11
  0.7 0.0 copy-start.8
  0.7 0.0 copy-start.9
  0.7 0.6 copy-done.10
  1.3 0.0 copy-done.11
  1.3 0.0 copy-done.8
  1.3 0.0 copy-done.9
  1.3 0.0 copy-start
  1.4 1.2 %copy-done = f32[8,64,448]{2,1,0:T(8,128)S(1)} copy-done((f32[8,64,448]{2,1,0:T(8,128)S(1)}, f32[8,64,448]{2,1,0:T(8,128)}, u32[]{:S(2)}) %copy-start) | copy-done | bytes 917528
  2.6 0.0 copy-start.1
  2.6 0.9 %copy-done.1 = bf16[8,64,128]{2,1,0:T(8,128)(2,1)S(1)} copy-done((bf16[8,64,128]{2,1,0:T(8,128)(2,1)S(1)}, bf16[8,64,128]{2,1,0:T(8,128)(2,1)}, u32[]{:S(2)}) %copy-start.1) | copy-done | bytes 131096
  3.5 0.0 copy-start.2
  3.5 0.9 %copy-done.2 = f32[8,64,64]{2,1,0:T(8,128)S(1)} copy-done((f32[8,64,64]{2,1,0:T(8,128)S(1)}, f32[8,64,64]{2,1,0:T(8,128)}, u32[]{:S(2)}) %copy-start.2) | copy-done | bytes 131096
  4.4 0.0 copy-start.3
  4.4 0.8 copy-done.3
  5.2 0.0 copy-start.4
  5.2 0.8 copy-done.4
  5.9 0.0 copy-start.5
  5.9 0.7 copy-done.5
  6.6 0.0 copy-start.6
  6.6 0.7 copy-done.6
  7.3 0.0 copy-start.7
  7.3 0.7 copy-done.7
  8.0 77.8 %shard_map.131 = (f32[8,64,128]{2,1,0:T(8,128)S(1)}, f32[8,64,128]{2,1,0:T(8,128)S(1)}, f32[8,128]{1,0:T(8,128)S(1)}) custom-call(s32[8,6]{1,0:T(8,128)S(1)} %copy-done.7, s32[8]{0:T(128)S(1)} %copy-done.9, s32[2,6]{1,0:T(2,128)S(1)} %copy-done.8, s32[2]{0:T(128)S(1)} %copy-done.10, s32[1,8]{1,0:T(1,128)S(1)} %copy-done.11, ...), custom_call_target="tpu_custom_call" | custom-call | tf_op jit(solution)/shard_map/pallas_call | solution.py:683
  85.8 0.8 multiply_subtract_fusion
  (1 shorter events, 0.0 us)
Async XLA Ops:
  0.6 0.7 copy-start.10
  0.6 0.7 copy-start.11
  0.7 0.7 copy-start.8
  0.7 0.7 copy-start.9
  1.3 1.2 %copy-start = (f32[8,64,448]{2,1,0:T(8,128)S(1)}, f32[8,64,448]{2,1,0:T(8,128)}, u32[]{:S(2)}) copy-start(f32[8,64,448]{2,1,0:T(8,128)} %blocks_hbm.1) | copy-start | bytes 2752516
  2.6 0.9 %copy-start.1 = (bf16[8,64,128]{2,1,0:T(8,128)(2,1)S(1)}, bf16[8,64,128]{2,1,0:T(8,128)(2,1)}, u32[]{:S(2)}) copy-start(bf16[8,64,128]{2,1,0:T(8,128)(2,1)} %rhs_hbm.1) | copy-start | bytes 393220
  3.5 0.9 %copy-start.2 = (f32[8,64,64]{2,1,0:T(8,128)S(1)}, f32[8,64,64]{2,1,0:T(8,128)}, u32[]{:S(2)}) copy-start(f32[8,64,64]{2,1,0:T(8,128)} %inverses_hbm.1) | copy-start | bytes 393220
  4.4 0.8 copy-start.3
  5.2 0.8 copy-start.4
  5.9 0.7 copy-start.5
  6.6 0.7 copy-start.6
  7.3 0.7 copy-start.7

commit v4 on v3

--- a/solution.py
+++ b/solution.py
@@ -174,7 +174,7 @@
             pl.semaphore_signal(barrier, inc=1, device_id=partner(i), device_id_type=MESH)
             return carry
 
-        lax.fori_loop(1, count, body, 0)
+        lax.fori_loop(1, count, body, 0, unroll=True)
 
     greet(lambda i: gather_partner(i)[0], SPAN * ngrp)
 
@@ -511,10 +511,9 @@
             y = y + d
         return y
 
-    held = 16 * (2 * SIDE + 1)
-    start = (REACH * ngrp + grp - SIDE) * 16
-    unit = (iota((128, full), 1) == iota((128, full), 0) + start) & (iota((128, full), 0) < held)
-    unit = unit.astype(F32)
+    shape = strip.shape
+    start = (REACH * ngrp + grp - SIDE - 1) * 16
+    unit = (iota(shape, 1) == iota(shape, 0) + start).astype(F32)
     u = smooth(unit)
     v = exact(u, kmat[...])
     strip[...] = v
@@ -525,12 +524,6 @@
     own_b[...] = mine_b - (share_landed[0, 0] + share_landed[0, 1])
     gather(own_b, all_b, b_send, b_recv, 1, SPAN * ngrp)
     all_b[REACH * ngrp + grp] = own_b[...]
-
-    local_step(da, update)
-    unit = (iota((128, full), 1) == iota((128, full), 0) + start) & (iota((128, full), 0) < held)
-    m = exact(unit.astype(F32) - strip[...], cmat[...])
-    y = smooth(strip[...] + exact(m, amat[...]))
-    strip[...] = m + exact(left[...] - y, dmat[...])
 
     def post_first(e, value):
         q0 = update[e]
@@ -541,7 +534,9 @@
         direction[e] = d1
         answer[e] = answer[e] + d0 + d1
 
+    local_step(da, update)
     finish_step(3, copies, da, post_first)
+    copies = exchange(4, direction)
 
     for e in range(ELEMS):
         one, two = m_one[e], m_two[e]
@@ -552,30 +547,49 @@
         m_one[e] = step
         m_two[e] = h
         m_three[e] = whole
+    copies_m.append(exchange_m(3, m_one))
+
+    m = exact(unit - strip[...], cmat[...])
+    y = smooth(strip[...] + exact(m, amat[...]))
+    strip[...] = m + exact(left[...] - y, dmat[...])
+
+    arrive(copies_m[3])
+    reach = 16 * (2 * SIDE + 1)
+    rest = jnp.zeros((LOADS - reach, HALO * NODES), F32)
+    for side in range(2):
+        tall = jnp.concatenate([m_landed[3, side, 0:reach], rest], axis=0).T
+        for j in range(HALO):
+            field[side * HALO + j] = tall[NODES * j : NODES * j + NODES]
 
     wait_bytes(all_b, gathered, b_recv)
     values = all_b[...].reshape(wide, LOADS)
     padded = jnp.concatenate([values, jnp.zeros((full - wide, LOADS), F32)], axis=0)
     c = exact(strip[...], padded)
+    rest = jnp.zeros((LOADS - reach, LOADS), F32)
+    c_before, c_own, c_after = (
+        jnp.concatenate([c[16 * i : 16 * i + reach], rest], axis=0) for i in range(3)
+    )
     rows = ELEMS * NODES
-    change = exact(m_one[...].reshape(rows, LOADS), c).reshape(ELEMS, NODES, LOADS)
+    change = exact(m_one[...].reshape(rows, LOADS), c_own).reshape(ELEMS, NODES, LOADS)
     direction[...] = direction[...] - change
 
-    copies = exchange(4, direction)
-    change = exact(m_two[...].reshape(rows, LOADS), c).reshape(ELEMS, NODES, LOADS)
+    arrive(copies)
+    for side, c_side in enumerate((c_before, c_after)):
+        some = field[side * HALO : side * HALO + HALO].reshape(HALO * NODES, LOADS)
+        change = exact(some, c_side).reshape(HALO, NODES, LOADS)
+        for j in range(HALO):
+            store_pieces(halo, side * HALO + j, landed[4, side, j] - change[j])
+    change = exact(m_two[...].reshape(rows, LOADS), c_own).reshape(ELEMS, NODES, LOADS)
     update[...] = update[...] - change
-    change = exact(m_three[...].reshape(rows, LOADS), c).reshape(ELEMS, NODES, LOADS)
+    change = exact(m_three[...].reshape(rows, LOADS), c_own).reshape(ELEMS, NODES, LOADS)
     answer[...] = answer[...] + change
-    local_step(da, direction)
+    cut(direction, window)
+    for e in range(ELEMS):
+        q = update[e] - (local_part(da, e, window) + halo_part(da, e, halo))
+        answer[e] = answer[e] + (KEEP[2] * direction[e] + TAKE[2] * q)
+
+    copies = exchange(5, answer)
     wait_bytes(all_b, gathered, b_send)
-
-    def post_last(e, value):
-        q = update[e] - value
-        answer[e] = answer[e] + (KEEP[2] * direction[e] + TAKE[2] * q)
-
-    finish_step(4, copies, da, post_last)
-
-    copies = exchange(5, answer)
     local_step(a, answer)
     sums = [jnp.zeros((8, LOADS), F32), jnp.zeros((8, LOADS), F32)]
     for e in range(ELEMS):
@@ -660,13 +674,13 @@
         pltpu.VMEM(shape, F32),
         pltpu.VMEM((ELEMS, 16, NODES), F32),
         *([pltpu.VMEM(shape, F32)] * 3),
-        *([pltpu.VMEM((3, 2, 16 * (2 * SIDE - 1), HALO * NODES), F32)] * 2),
+        *([pltpu.VMEM((4, 2, 16 * (2 * SIDE + 1), HALO * NODES), F32)] * 2),
         *([pltpu.VMEM((1, 2, 16, HALO * NODES), F32)] * 2),
         *([pltpu.VMEM((1, 2, 16, LOADS), F32)] * 2),
         pltpu.VMEM((16, LOADS), F32),
         pltpu.VMEM((held, 16, LOADS), F32),
         *([pltpu.VMEM((full, full), F32)] * 4),
-        *([pltpu.VMEM((128, full), F32)] * 2),
+        *([pltpu.VMEM((16 * (2 * SIDE + 3), full), F32)] * 2),
         pltpu.VMEM((16, LOADS), F32),
         pltpu.VMEM((held, 16, LOADS), F32),
         pltpu.VMEM((8, LOADS), F32),
@@ -675,7 +689,7 @@
         pltpu.VMEM((ngy, 8, LOADS), F32),
         pltpu.SemaphoreType.DMA((4,)),
         *([pltpu.SemaphoreType.DMA((exchanges, 2))] * 2),
-        *([pltpu.SemaphoreType.DMA((3, 2))] * 2),
+        *([pltpu.SemaphoreType.DMA((4, 2))] * 2),
         *([pltpu.SemaphoreType.DMA((1, 2))] * 4),
         *([pltpu.SemaphoreType.DMA] * 4),
         *([pltpu.SemaphoreType.DMA((2,))] * 2),

time: 87.1 us -> 86.8 us (level)
  no operation moved by 1% of the time
where the time goes in v4:
time: 86.8 us; the launch traced here: 86.4 us
  Pallas kernels  77.5 us (89%)
  local copies, waits for them, and re-layouts  7.36 us (8%)
    pallas_call x1, Pallas kernels, on_device(): pl.pallas_call(functools.partial(kernel, sizes), out_shape=(jax.ShapeDtyp...  77.5 us
    unnamed x24, local copies, waits for them, and re-layouts  7.35 us

profile of v4, /device:TPU:1, one launch (start us, length us, event | category | flops | bytes accessed | tf_op | source)
XLA Modules:
  0.0 86.4 jit_solution(8292773498091224962)
XLA Ops:
  0.6 0.0 copy-start.10
  0.6 0.0 copy-start.11
  0.7 0.0 copy-start.8
  0.7 0.0 copy-start.9
  0.7 0.6 copy-done.10
  1.3 0.0 copy-done.11
  1.3 0.0 copy-done.8
  1.3 0.0 copy-done.9
  1.3 0.0 copy-start
  1.4 1.2 %copy-done = f32[8,64,448]{2,1,0:T(8,128)S(1)} copy-done((f32[8,64,448]{2,1,0:T(8,128)S(1)}, f32[8,64,448]{2,1,0:T(8,128)}, u32[]{:S(2)}) %copy-start) | copy-done | bytes 917528
  2.6 0.0 copy-start.1
  2.6 0.9 %copy-done.1 = bf16[8,64,128]{2,1,0:T(8,128)(2,1)S(1)} copy-done((bf16[8,64,128]{2,1,0:T(8,128)(2,1)S(1)}, bf16[8,64,128]{2,1,0:T(8,128)(2,1)}, u32[]{:S(2)}) %copy-start.1) | copy-done | bytes 131096
  3.5 0.0 copy-start.2
  3.5 0.9 %copy-done.2 = f32[8,64,64]{2,1,0:T(8,128)S(1)} copy-done((f32[8,64,64]{2,1,0:T(8,128)S(1)}, f32[8,64,64]{2,1,0:T(8,128)}, u32[]{:S(2)}) %copy-start.2) | copy-done | bytes 131096
  4.4 0.0 copy-start.3
  4.4 0.8 copy-done.3
  5.2 0.0 copy-start.4
  5.2 0.8 copy-done.4
  5.9 0.0 copy-start.5
  5.9 0.7 copy-done.5
  6.6 0.0 copy-start.6
  6.6 0.7 copy-done.6
  7.3 0.0 copy-start.7
  7.3 0.7 copy-done.7
  8.0 77.5 %shard_map.131 = (f32[8,64,128]{2,1,0:T(8,128)S(1)}, f32[8,64,128]{2,1,0:T(8,128)S(1)}, f32[8,128]{1,0:T(8,128)S(1)}) custom-call(s32[8,6]{1,0:T(8,128)S(1)} %copy-done.7, s32[8]{0:T(128)S(1)} %copy-done.9, s32[2,6]{1,0:T(2,128)S(1)} %copy-done.8, s32[2]{0:T(128)S(1)} %copy-done.10, s32[1,8]{1,0:T(1,128)S(1)} %copy-done.11, ...), custom_call_target="tpu_custom_call" | custom-call | tf_op jit(solution)/shard_map/pallas_call | solution.py:697
  85.5 0.8 multiply_subtract_fusion
  (1 shorter events, 0.0 us)
Async XLA Ops:
  0.6 0.7 copy-start.10
  0.6 0.7 copy-start.11
  0.7 0.7 copy-start.8
  0.7 0.7 copy-start.9
  1.3 1.2 %copy-start = (f32[8,64,448]{2,1,0:T(8,128)S(1)}, f32[8,64,448]{2,1,0:T(8,128)}, u32[]{:S(2)}) copy-start(f32[8,64,448]{2,1,0:T(8,128)} %blocks_hbm.1) | copy-start | bytes 2752516
  2.6 0.9 %copy-start.1 = (bf16[8,64,128]{2,1,0:T(8,128)(2,1)S(1)}, bf16[8,64,128]{2,1,0:T(8,128)(2,1)}, u32[]{:S(2)}) copy-start(bf16[8,64,128]{2,1,0:T(8,128)(2,1)} %rhs_hbm.1) | copy-start | bytes 393220
  3.5 0.9 %copy-start.2 = (f32[8,64,64]{2,1,0:T(8,128)S(1)}, f32[8,64,64]{2,1,0:T(8,128)}, u32[]{:S(2)}) copy-start(f32[8,64,64]{2,1,0:T(8,128)} %inverses_hbm.1) | copy-start | bytes 393220
  4.4 0.8 copy-start.3
  5.2 0.8 copy-start.4
  5.9 0.7 copy-start.5
  6.6 0.7 copy-start.6
  7.3 0.7 copy-start.7

commit v5 on v4

--- a/solution.py
+++ b/solution.py
@@ -705,7 +705,7 @@
         out_specs=(vmem, vmem, vmem),
         scratch_shapes=scratch,
         compiler_params=pltpu.CompilerParams(
-            collective_id=0, has_side_effects=True, vmem_limit_bytes=48 * 1024 * 1024
+            collective_id=0, has_side_effects=True, vmem_limit_bytes=64 * 1024 * 1024
         ),
     )(
         element_table,

time: 86.8 us -> 81.7 us (0.941)
  local copies, waits for them, and re-layouts: 7.36 us -> 0.68 us
  other arithmetic: 0.84 us -> 1.94 us
    unnamed x24 -> x0, local copies, waits for them, and re-layouts: 7.35 us -> none
    sub x1, other arithmetic: 0.84 us -> 1.94 us  [on_device(): return (step * x, rhs.astype(F32) - step * applied)]
where the time goes in v5:
time: 81.7 us; the launch traced here: 81.4 us
  Pallas kernels  78.1 us (96%)
  other arithmetic  1.94 us (2%)
    pallas_call x1, Pallas kernels, on_device(): pl.pallas_call(functools.partial(kernel, sizes), out_shape=(jax.ShapeDtyp...  78.1 us
    sub x1, other arithmetic, on_device(): return (step * x, rhs.astype(F32) - step * applied)  1.94 us

profile of v5, /device:TPU:1, one launch (start us, length us, event | category | flops | bytes accessed | tf_op | source)
XLA Modules:
  0.0 81.4 jit_solution(14998270788025787014)
XLA Ops:
  0.6 78.1 %shard_map.131 = (f32[8,64,128]{2,1,0:T(8,128)}, f32[8,64,128]{2,1,0:T(8,128)}, f32[8,128]{1,0:T(8,128)}) custom-call(s32[8,6]{1,0:T(8,128)} %table.1, s32[8]{0:T(128)} %member.1, s32[2,6]{1,0:T(2,128)} %coarse_table.1, s32[2]{0:T(128)} %coarse_map.1, s32[1,8]{1,0:T(1,128)} %owner.1, bf16[8,64,128]{2,1,0:T(8,128)(2,1)} %rhs_hbm.1, ...), custom_call_target="tpu_custom_call" | custom-call | tf_op jit(solution)/shard_map/pallas_call | solution.py:697
  78.8 0.7 slice_bitcast_fusion
  79.5 1.9 %multiply_subtract_fusion = (f32[8,64,128]{2,1,0:T(8,128)}, f32[8,64,128]{2,1,0:T(8,128)}) fusion(f32[8,64,128]{2,1,0:T(8,128)} %get-tuple-element.7, bf16[8,64,128]{2,1,0:T(8,128)(2,1)} %rhs_hbm.1, f32[128]{0:T(128)S(1)} %slice_bitcast_fusion, f32[8,64,128]{2,1,0:T(8,128)} %get-tuple-element.6), kind=kLoop, calls=%fused_computation | loop fusion | flops 262144 | bytes 1180160 | tf_op jit(solution)/shard_map/sub | solution.py:725
